TPU v7x, 512 devices: a whole 4x8x8 slice. The times are simulated.
512 devices in a mesh: pipe: 8 (over z), mp: 16 (over y, core), dp: 4 (over x).
Axes of the slice: x: 4, y: 8, z: 8, core: 2. Of those that a mesh axis runs over, the one named last changes fastest.
Arguments:
- hidden: bfloat16 [49152, 8192], P(('pipe', 'dp'), 'mp'), may hold values from -6 to 6
- latent_head_weight: bfloat16 [8192, 512], P('mp', 'dp'), may hold values from -0.0625 to 0.0625
- stretch_holder: int32 [2048, 2], P(('pipe', 'dp')), may hold values from 0 to 15, as said below
- stretch_position: int32 [2048, 2], P(('pipe', 'dp')), may hold values from 0 to 15, as said below
- stretch_frame_count: int32 [2048, 2], P(('pipe', 'dp')), may hold values from 1 to 12
- upsample_weight: bfloat16 [2, 512, 2048], P(None, 'dp'), may hold values from -0.1875 to 0.1875
- upsample_bias: float32 [256], replicated, may hold values from -3 to 3
- snake_alpha_first: float32 [256], replicated, may hold values from 0.5 to 4
- dilated_weight: bfloat16 [3, 256, 256], replicated, may hold values from -0.21875 to 0.21875
- snake_alpha_second: float32 [256], replicated, may hold values from 0.5 to 4
- pointwise_weight: bfloat16 [256, 256], replicated, may hold values from -0.375 to 0.375
Outputs:
- vocoded: bfloat16 [8, 256, 4, 96, 256], P('pipe', 'mp', 'dp')
Inputs may be any that keep to these rules, and one draw needn't show every extreme that they name: `stretch_holder`: streams g * 64 to (g + 1) * 64 - 1 form vocoder group g. In each group every owner is named by at most 16 stretches, and one owner by exactly 16. The 8 stretches of each aligned block of 4 streams of a group name one owner at most 2 times, and some block does so exactly 2 times. `stretch_position`: within a group, the stretches of one owner hold the slots 0 up to their number minus one, each once.
All inputs are finite; a program needn't handle non-finite values.
Results may differ from a plain program's by a relative error of at most 0.007.
Values may be sent and summed in bfloat16 or wider, within the bound.
A program may use at most 64 MiB of HBM per device.

v0:
```python
import jax
import jax.numpy as jnp
from jax import lax
from jax.sharding import PartitionSpec as P

DILATION_RATE = 3
CTX = 2


def snake_act(signal, alpha_rate):
    return signal + jnp.sin(alpha_rate * signal) ** 2 / alpha_rate


def item_layout(counts, frames_item, stretch_len):
    stream_total = counts.shape[0]
    context = frames_item - stretch_len
    frame_place = jnp.arange(frames_item, dtype=jnp.int32)[None, :]
    stretch_frame = jnp.broadcast_to(frame_place - context, (stream_total, frames_item))
    first_count = counts[:, 0:1]
    second = counts[:, 1:2]
    alive_first = (stretch_frame >= 0) & (stretch_frame < first_count)
    rows_second = jnp.where(
        stretch_frame < 0, first_count + stretch_frame, stretch_len + stretch_frame
    )
    alive_second = jnp.where(
        stretch_frame < 0, first_count + stretch_frame >= 0, stretch_frame < second
    )
    item_rows = jnp.clip(jnp.stack([stretch_frame, rows_second], axis=1), 0, 2 * stretch_len - 1)
    item_active_mask = jnp.stack([alive_first, alive_second], axis=1)
    return (item_rows, item_active_mask)


def vocoder_forward(
    stretch_items,
    item_active_mask,
    upsample_weight,
    upsample_bias,
    snake_alpha_first,
    dilated_weight,
    snake_alpha_second,
    pointwise_weight,
):
    item_count, length, latent_width = stretch_items.shape
    up_width = upsample_bias.shape[0]
    stride_len = upsample_weight.shape[2] // up_width
    flat_items = stretch_items.reshape(item_count * length, latent_width)
    before = jnp.concatenate(
        [jnp.zeros((item_count, 1, latent_width), stretch_items.dtype), stretch_items[:, :-1]],
        axis=1,
    )
    before = before.reshape(item_count * length, latent_width)
    weight_piece = lax.all_gather(upsample_weight, "dp", axis=1, tiled=True)
    running = jnp.dot(flat_items, weight_piece[0], preferred_element_type=jnp.float32)
    upsampled = running + jnp.dot(before, weight_piece[1], preferred_element_type=jnp.float32)
    upsampled = upsampled.reshape(item_count, length, stride_len, up_width) + upsample_bias
    upsampled = upsampled * item_active_mask.astype(jnp.float32)[:, :, None, None]
    upsampled = upsampled.reshape(item_count, length * stride_len, up_width)
    first_activation = snake_act(upsampled, snake_alpha_first).astype(jnp.bfloat16)
    output_start = CTX * stride_len
    out_span = (length - CTX) * stride_len
    dilated_output = jnp.zeros((item_count, out_span, up_width), jnp.float32)
    for kernel_tap_index in range(3):
        frame_offset = output_start - kernel_tap_index * DILATION_RATE
        kernel_tap_input = lax.slice_in_dim(
            first_activation, frame_offset, frame_offset + out_span, axis=1
        )
        dilated_output = dilated_output + jnp.einsum(
            "fgo,op->fgp",
            kernel_tap_input,
            dilated_weight[kernel_tap_index],
            preferred_element_type=jnp.float32,
        )
    second_act = snake_act(dilated_output, snake_alpha_second).astype(jnp.bfloat16)
    pointwise = jnp.einsum(
        "fgo,op->fgp", second_act, pointwise_weight, preferred_element_type=jnp.float32
    )
    kept_mask = jnp.repeat(item_active_mask[:, CTX:], stride_len, axis=1)
    return jnp.where(kept_mask[:, :, None], upsampled[:, output_start:] + pointwise, 0.0).astype(
        jnp.bfloat16
    )


def body(
    hidden,
    latent_head_weight,
    stretch_holder,
    stretch_position,
    stretch_frame_count,
    upsample_weight,
    upsample_bias,
    snake_alpha_first,
    dilated_weight,
    snake_alpha_second,
    pointwise_weight,
):
    peer_count = lax.axis_size("mp")
    self_index = lax.axis_index("mp")
    head_weight = lax.all_gather(latent_head_weight, "dp", axis=1, tiled=True)
    own_rows = hidden.shape[0] // peer_count
    latent = lax.psum_scatter(
        jnp.dot(hidden, head_weight, preferred_element_type=jnp.float32),
        "mp",
        scatter_dimension=0,
        tiled=True,
    ).astype(jnp.bfloat16)
    group_streams = stretch_frame_count.shape[0]
    per_device = group_streams // peer_count
    seq_len = own_rows // per_device
    stretch_len = seq_len // 2
    frames_item = stretch_len + CTX
    latent_width = latent.shape[1]
    up_width = upsample_bias.shape[0]
    samples = stretch_len * (upsample_weight.shape[2] // up_width)
    item_rows, item_active_mask = item_layout(stretch_frame_count, frames_item, stretch_len)
    my_rows = lax.dynamic_slice_in_dim(item_rows, self_index * per_device, per_device, 0)
    my_rows = my_rows.reshape(per_device, 2 * frames_item)
    my_alive = lax.dynamic_slice_in_dim(item_active_mask, self_index * per_device, per_device, 0)
    my_alive = my_alive.reshape(2 * per_device, frames_item)
    stream_latent = latent.reshape(per_device, seq_len, latent_width)
    picked = jnp.take_along_axis(stream_latent, my_rows[:, :, None], axis=1)
    picked = picked.reshape(2 * per_device, frames_item, latent_width)
    my_items = jnp.where(my_alive[:, :, None], picked, jnp.zeros((), jnp.bfloat16))
    owner_list = stretch_holder.reshape(-1)
    slot_list = stretch_position.reshape(-1)
    item_total = owner_list.shape[0]
    items_device = 2 * per_device
    recv_cap = 2 * items_device
    send_cap = 2 * ((items_device + peer_count - 1) // peer_count)
    item_order = jnp.arange(item_total, dtype=jnp.int32)
    source = item_order // items_device
    earlier = (source[:, None] == source[None, :]) & (owner_list[:, None] == owner_list[None, :])
    earlier = earlier & (item_order[None, :] < item_order[:, None])
    send_slot = jnp.sum(earlier.astype(jnp.int32), axis=1)
    position = source * send_cap + send_slot
    target = owner_list * send_cap + send_slot
    matched = (
        (owner_list[None, :] == self_index)
        & (slot_list[None, :] == jnp.arange(recv_cap, dtype=jnp.int32)[:, None])
    ).astype(jnp.int32)
    chosen_item = jnp.sum(matched * item_order[None, :], axis=1)
    present = jnp.sum(matched, axis=1) > 0
    fetch_index = jnp.sum(matched * position[None, :], axis=1)
    my_target = lax.dynamic_slice_in_dim(target, self_index * items_device, items_device, 0)
    outgoing = (
        jnp.zeros((peer_count * send_cap, frames_item, latent_width), jnp.bfloat16)
        .at[my_target]
        .set(my_items)
    )
    outgoing = outgoing.reshape(peer_count, send_cap * frames_item, latent_width)
    arrived = lax.all_to_all(outgoing, "mp", split_axis=0, concat_axis=0, tiled=True)
    arrived = arrived.reshape(peer_count * send_cap, frames_item, latent_width)
    slot_entries = arrived[fetch_index]
    slot_active_mask = (
        item_active_mask.reshape(item_total, frames_item)[chosen_item] & present[:, None]
    )
    unit_output = vocoder_forward(
        slot_entries,
        slot_active_mask,
        upsample_weight,
        upsample_bias,
        snake_alpha_first,
        dilated_weight,
        snake_alpha_second,
        pointwise_weight,
    )
    return unit_output.reshape(1, recv_cap, 1, samples, up_width)


def solution(mesh):
    in_specs = (
        P(("pipe", "dp"), "mp"),
        P("mp", "dp"),
        P(("pipe", "dp"), None),
        P(("pipe", "dp"), None),
        P(("pipe", "dp"), None),
        P(None, "dp", None),
        P(),
        P(),
        P(),
        P(),
        P(),
    )
    out_specs = P("pipe", "mp", "dp", None, None)
    return jax.shard_map(body, mesh=mesh, in_specs=in_specs, out_specs=out_specs, check_vma=False)
```

profile of v0, /device:TPU:1, one launch (start us, length us, event | category | flops | bytes accessed | tf_op | source)
XLA Modules:
  0.0 157.2 jit_solution(17077849503522527697)
XLA Ops:
  7.4 0.0 copy-start
  7.4 0.0 reduce-scatter.2.cloned.1.call-start
  7.4 13.3 %all_gather.6 = bf16[512,512]{1,0:T(8,128)(2,1)S(1)} all-gather(bf16[512,128]{1,0:T(8,128)(2,1)} %param.12), channel_id=1, replica_groups=mesh['pipe'=8,'mp'=16,'dp'=4] {'dp'}, dimensions={1}, use_global_device_ids=true | all-gather | bytes 655360 | tf_op jit(solution)/shard_map/all_gather | solution.py:98
  20.6 0.0 copy-done
  20.6 2.6 %fusion.31 = f32[1536,512]{1,0:T(8,128)} fusion(bf16[1536,512]{1,0:T(8,128)(2,1)S(1)} %copy-done, bf16[512,512]{1,0:T(8,128)(2,1)S(1)} %all_gather.6), kind=kOutput, calls=%fused_computation.77 | convolution fusion | flops 805306368 | bytes 5242880 | tf_op jit(solution)/shard_map/dot_general | solution.py:101
  23.3 0.0 reduce-scatter.2.cloned.1.call-update
  23.3 0.0 all-gather.2.cloned.1.call-start
  23.4 0.5 all-gather.2.cloned.1.call-update
  23.9 0.0 copy-done.6
  24.0 0.1 compare_and_fusion
  24.0 0.1 fusion.21
  24.1 0.1 copy.40
  24.3 0.1 add_select_fusion
  24.4 0.1 broadcast_in_dim.83.clone
  24.4 0.1 fusion.22
  24.6 0.1 copy.43
  24.7 0.1 broadcast_in_dim_reshape.15
  24.7 0.1 reshape.457
  24.8 0.0 copy-done.4
  24.8 0.1 copy.36
  24.9 0.1 broadcast_in_dim_reshape.6
  25.1 0.0 copy-done.5
  25.1 0.1 copy.37
  25.2 0.1 eq.54
  25.3 0.1 copy.35
  25.5 0.2 convert_reduce_fusion
  25.7 0.1 convert_reduce_fusion.1
  25.9 0.6 gather_fusion
  26.5 0.1 compare_select_fusion.3
  26.6 65.9 %reduce-scatter.2.cloned.1.call-done = f32[96,512]{1,0:T(8,128)} async-done(((f32[1536,512]{1,0:T(8,128)}), f32[96,512]{1,0:T(8,128)}) %reduce-scatter.2.cloned.1.call-update) | async-done | bytes 196624 | tf_op jit(solution)/shard_map/reduce_scatter | solution.py:100
  92.5 0.9 convert_element_type.27
  93.4 1.7 %gather_fusion.2 = bf16[112,512]{1,0:T(8,128)(2,1)S(1)} fusion(bf16[4,24,512]{2,1,0:T(8,128)(2,1)S(1)} %bitcast.51, s32[112]{0:T(128)S(1)} %reshape.457), kind=kCustom, calls=%fused_computation.2 | custom fusion | bytes 230272 | tf_op jit(solution)/shard_map/jit(take_along_axis)/gather | solution.py:120
  95.1 0.1 select_select_fusion
  95.2 0.1 broadcast_in_dim.88
  95.3 0.7 scatter_fusion
  96.0 0.9 reshape.435
  96.9 7.0 %all-to-all-start = ((bf16[16,28,512]{2,1,0:T(8,128)(2,1)}), bf16[16,28,512]{2,1,0:T(8,128)(2,1)S(1)}, u32[]{:S(2)}, u32[]{:S(2)}) async-start(bf16[16,28,512]{2,1,0:T(8,128)(2,1)} %reshape.435), calls=%async_computation.1 | async-start | bytes 1048576 | tf_op jit(solution)/shard_map/all_to_all | solution.py:150
  103.9 0.1 fusion.30
  104.0 0.1 copy.45
  104.1 0.1 copy.46
  104.2 0.1 slice.64
  104.2 0.1 copy.38
  104.4 0.1 copy.39
  104.5 16.8 %all-to-all-done = bf16[16,28,512]{2,1,0:T(8,128)(2,1)S(1)} async-done(((bf16[16,28,512]{2,1,0:T(8,128)(2,1)}), bf16[16,28,512]{2,1,0:T(8,128)(2,1)S(1)}, u32[]{:S(2)}, u32[]{:S(2)}) %all-to-all-start) | async-done | bytes 458784 | tf_op jit(solution)/shard_map/all_to_all | solution.py:150
  121.3 0.1 reshape.436
  121.4 0.6 gather_fusion.1
  121.9 0.1 reshape.437
  122.0 0.1 concatenate.3
  122.1 0.1 reshape.438
  122.2 0.0 all-gather.2.cloned.1.call-done
  122.2 2.2 %fusion = f32[224,2048]{1,0:T(8,128)S(1)} fusion(bf16[224,512]{1,0:T(8,128)(2,1)S(1)} %reshape.437, bf16[2,512,2048]{2,1,0:T(8,128)(2,1)} %all-gather.2.cloned.1.call-done), kind=kOutput, calls=%fused_computation.7 | convolution fusion | flops 469762048 | bytes 4161536 | tf_op jit(solution)/shard_map/dot_general | solution.py:53
  124.5 3.6 %convolution_add_fusion = f32[224,2048]{1,0:T(8,128)} fusion(f32[224,2048]{1,0:T(8,128)S(1)} %fusion, bf16[224,512]{1,0:T(8,128)(2,1)S(1)} %reshape.438, bf16[2,512,2048]{2,1,0:T(8,128)(2,1)} %all-gather.2.cloned.1.call-done), kind=kOutput, calls=%fused_computation.4 | convolution fusion | flops 470220800 | bytes 5996544 | tf_op jit(solution)/shard_map/dot_general | solution.py:54
  128.0 1.6 %reshape.439 = f32[16,112,256]{2,1,0:T(8,128)S(1)} reshape(f32[224,2048]{1,0:T(8,128)} %convolution_add_fusion) | data formatting | bytes 3670016 | tf_op jit(solution)/shard_map/reshape | solution.py:55
  129.6 0.0 copy-done.7
  129.7 0.0 copy-done.8
  129.7 0.0 copy-start.3
  129.7 7.6 %add_convert_fusion = (bf16[16,112,256]{2,1,0:T(8,128)(2,1)S(1)}, f32[16,112,256]{2,1,0:T(8,128)}) fusion(f32[256]{0:T(256)S(1)} %copy-done.7, f32[16,112]{1,0:T(8,128)S(1)} %copy.46, f32[16,112,256]{2,1,0:T(8,128)S(1)} %reshape.439, f32[256]{0:T(256)S(1)} %copy-done.8), kind=kLoop, calls=%fused_computation.8 | loop fusion | flops 3211264 | bytes 4596736 | tf_op jit(solution)/shard_map/convert_element_type | solution.py:58
  137.3 0.0 copy-done.3
  137.3 1.6 fusion.5
  138.8 1.5 fusion.7
  140.3 0.0 copy-done.1
  140.3 0.4 copy-done.2
  140.7 0.1 copy-done.9
  140.8 9.0 %fusion.3 = bf16[1,16,1,96,256]{4,3,2,1,0:T(8,128)(2,1)} fusion(f32[16,112,256]{2,1,0:T(8,128)S(1)} %copy-done.2, pred[16,96]{1,0:T(8,128)(4,1)S(1)} %copy.39, f32[16,96,256]{2,1,0:T(8,128)} %fusion.7, f32[16,96,256]{2,1,0:T(8,128)} %fusion.5, bf16[16,112,256]{2,1,0:T(8,128)(2,1)} %copy-done.1, f32[256]{0:T(256)S(1)} %copy-done.10, ...), kind=kOutput, calls=%fused_computation.14 | convolution fusion | flops 406585344 | bytes 6556160 | tf_op jit(solution)/shard_map/fgo,op->fgp/dot_general | solution.py:74
  (30 shorter events, 0.3 us)
Async XLA Ops:
  7.4 13.3 %copy-start = (bf16[1536,512]{1,0:T(8,128)(2,1)S(1)}, bf16[1536,512]{1,0:T(8,128)(2,1)}, u32[]{:S(2)}) copy-start(bf16[1536,512]{1,0:T(8,128)(2,1)} %param.11) | copy-start | bytes 4718596
  7.4 85.1 %reduce-scatter.2.cloned.1.call-start = ((), (), s32[]{:S(2)}) async-start(), calls=%async_computation.2 | async-start | bytes 3342336 | tf_op jit(solution)/shard_map/reduce_scatter | solution.py:100
  23.3 0.7 copy-start.6
  23.3 1.6 copy-start.4
  23.3 1.8 %copy-start.5 = (s32[64,2]{0,1:T(2,128)S(1)}, s32[64,2]{0,1:T(2,128)}, u32[]{:S(2)}) copy-start(s32[64,2]{0,1:T(2,128)} %param.14) | copy-start | bytes 1540
  23.3 98.9 %all-gather.2.cloned.1.call-start = ((), (), s32[]{:S(2)}) async-start(), calls=%async_computation.3 | async-start | bytes 5242880 | tf_op jit(solution)/shard_map/all_gather | solution.py:52
  96.9 24.3 %all-to-all-start = ((bf16[16,28,512]{2,1,0:T(8,128)(2,1)}), bf16[16,28,512]{2,1,0:T(8,128)(2,1)S(1)}, u32[]{:S(2)}, u32[]{:S(2)}) async-start(bf16[16,28,512]{2,1,0:T(8,128)(2,1)} %reshape.435), calls=%async_computation.1 | async-start | bytes 1048576 | tf_op jit(solution)/shard_map/all_to_all | solution.py:150
  128.0 1.6 %copy-start.7 = (f32[256]{0:T(256)S(1)}, f32[256]{0:T(256)}, u32[]{:S(2)}) copy-start(f32[256]{0:T(256)} %param.18) | copy-start | bytes 3076
  128.0 1.6 %copy-start.8 = (f32[256]{0:T(256)S(1)}, f32[256]{0:T(256)}, u32[]{:S(2)}) copy-start(f32[256]{0:T(256)} %param.17) | copy-start | bytes 3076
  129.7 7.6 %copy-start.3 = (bf16[3,256,256]{2,1,0:T(8,128)(2,1)S(1)}, bf16[3,256,256]{2,1,0:T(8,128)(2,1)}, u32[]{:S(2)}) copy-start(bf16[3,256,256]{2,1,0:T(8,128)(2,1)} %param.19) | copy-start | bytes 1179652
  137.3 3.1 %copy-start.1 = (bf16[16,112,256]{2,1,0:T(8,128)(2,1)}, bf16[16,112,256]{2,1,0:T(8,128)(2,1)S(1)}, u32[]{:S(2)}) copy-start(bf16[16,112,256]{2,1,0:T(8,128)(2,1)S(1)} %get-tuple-element.8) | copy-start | bytes 2752516
  138.8 1.9 %copy-start.2 = (f32[16,112,256]{2,1,0:T(8,128)S(1)}, f32[16,112,256]{2,1,0:T(8,128)}, u32[]{:S(2)}) copy-start(f32[16,112,256]{2,1,0:T(8,128)} %get-tuple-element.9) | copy-start | bytes 5505028
  138.8 2.0 %copy-start.9 = (bf16[256,256]{1,0:T(8,128)(2,1)S(1)}, bf16[256,256]{1,0:T(8,128)(2,1)}, u32[]{:S(2)}) copy-start(bf16[256,256]{1,0:T(8,128)(2,1)} %param.21) | copy-start | bytes 393220
  138.8 2.0 %copy-start.10 = (f32[256]{0:T(256)S(1)}, f32[256]{0:T(256)}, u32[]{:S(2)}) copy-start(f32[256]{0:T(256)} %param.20) | copy-start | bytes 3076
Sparse Core Ops, SparseCore 0:
  23.4 69.0 reduce-scatter.1
Sparse Core Ops, SparseCore 1:
  25.9 59.2 all-gather.1
where the time goes:
time: 158 us; the launch traced here: 157 us
  waiting for transfers between devices  83.2 us (53%)
  matrix products  20.4 us (13%)
  between operations  15.1 us (10%)
  blocking collectives  13.3 us (8%)
  other arithmetic  9.54 us (6%)
  local copies, waits for them, and re-layouts  8.56 us (5%)
  starting transfers between devices  7.04 us (4%)
    reduce_scatter x1, waiting for transfers between devices, body(): lax.psum_scatter(jnp.dot(hidden, head_weight, preferred_element_type=jnp....  65.9 us
    all_to_all x1, waiting for transfers between devices, body(): lax.all_to_all(outgoing, 'mp', split_axis=0, concat_axis=0, tiled=True)  16.8 us
    all_gather x1, blocking collectives, body(): head_weight = lax.all_gather(latent_head_weight, 'dp', axis=1, tiled=True)  13.3 us
    dot_general x1, matrix products, vocoder_forward(): jnp.einsum('fgo,op->fgp', second_act, pointwise_weight, preferred_element...  8.96 us
    convert_element_type x1, other arithmetic, vocoder_forward(): snake_act(upsampled, snake_alpha_first).astype(jnp.bfloat16)  7.58 us
    all_to_all x1, starting transfers between devices, body(): lax.all_to_all(outgoing, 'mp', split_axis=0, concat_axis=0, tiled=True)  6.99 us
    dot_general x1, matrix products, vocoder_forward(): jnp.dot(before, weight_piece[1], preferred_element_type=jnp.float32)  3.56 us
  transfers between devices with their start and end apart: 3, of which 2 were waited for; matrix products, arithmetic and copies ran while one was open for 5% of the time, Pallas kernels for 0%

commit v1 on v0

--- a/solution.py
+++ b/solution.py
@@ -1,14 +1,14 @@
+import functools
+
 import jax
 import jax.numpy as jnp
 from jax import lax
+from jax.experimental import pallas as pl
+from jax.experimental.pallas import tpu as pltpu
 from jax.sharding import PartitionSpec as P
 
 DILATION_RATE = 3
 CTX = 2
-
-
-def snake_act(signal, alpha_rate):
-    return signal + jnp.sin(alpha_rate * signal) ** 2 / alpha_rate
 
 
 def item_layout(counts, frames_item, stretch_len):
@@ -30,54 +30,112 @@
     return (item_rows, item_active_mask)
 
 
-def vocoder_forward(
-    stretch_items,
-    item_active_mask,
-    upsample_weight,
-    upsample_bias,
-    snake_alpha_first,
-    dilated_weight,
-    snake_alpha_second,
-    pointwise_weight,
-):
-    item_count, length, latent_width = stretch_items.shape
-    up_width = upsample_bias.shape[0]
-    stride_len = upsample_weight.shape[2] // up_width
-    flat_items = stretch_items.reshape(item_count * length, latent_width)
-    before = jnp.concatenate(
-        [jnp.zeros((item_count, 1, latent_width), stretch_items.dtype), stretch_items[:, :-1]],
-        axis=1,
-    )
-    before = before.reshape(item_count * length, latent_width)
-    weight_piece = lax.all_gather(upsample_weight, "dp", axis=1, tiled=True)
-    running = jnp.dot(flat_items, weight_piece[0], preferred_element_type=jnp.float32)
-    upsampled = running + jnp.dot(before, weight_piece[1], preferred_element_type=jnp.float32)
-    upsampled = upsampled.reshape(item_count, length, stride_len, up_width) + upsample_bias
-    upsampled = upsampled * item_active_mask.astype(jnp.float32)[:, :, None, None]
-    upsampled = upsampled.reshape(item_count, length * stride_len, up_width)
-    first_activation = snake_act(upsampled, snake_alpha_first).astype(jnp.bfloat16)
-    output_start = CTX * stride_len
-    out_span = (length - CTX) * stride_len
-    dilated_output = jnp.zeros((item_count, out_span, up_width), jnp.float32)
-    for kernel_tap_index in range(3):
-        frame_offset = output_start - kernel_tap_index * DILATION_RATE
-        kernel_tap_input = lax.slice_in_dim(
-            first_activation, frame_offset, frame_offset + out_span, axis=1
+SIN2 = (
+    9.869604110717773,
+    -32.469669342041016,
+    42.727195739746094,
+    -30.101465225219727,
+    13.05009937286377,
+    -3.3565926551818848,
+)
+
+
+def snake(v, turns, inverse):
+    u = v * turns
+    r = u - jnp.round(u)
+    s = r * r
+    q = jnp.full_like(s, SIN2[-1])
+    for c in SIN2[-2::-1]:
+        q = q * s + c
+    return v + (q * s) * inverse
+
+
+def vocode(slots, frames, stride, tab, x_ref, wup, bias, a1, dw, a2, pw, out_ref, up, act, out32):
+    rows = frames * slots
+    live = rows - 2 * slots
+    width = bias.shape[1]
+    half = width // 2
+    span = (frames - 2) * stride
+    lane = lax.broadcasted_iota(jnp.int32, (slots, width), 0)
+    count = jnp.zeros((slots, width), jnp.int32)
+    second = jnp.zeros((slots, width), jnp.int32)
+    for s in range(slots):
+        word = tab(s)
+        count = jnp.where(lane == s, (word // 2) % 16, count)
+        second = jnp.where(lane == s, (word // 256) % 2, second)
+    turns1 = a1[...] * (1.0 / jnp.pi)
+    inv1 = 1.0 / a1[...]
+    turns2 = a2[...] * (1.0 / jnp.pi)
+    inv2 = 1.0 / a2[...]
+    x1 = x_ref[pl.ds(slots, rows - slots), :]
+    x0 = x_ref[pl.ds(0, rows - slots), :]
+
+    def first(r, carry):
+        col = pl.ds(pl.multiple_of(r * width, width), width)
+        u = jnp.dot(x1, wup[0, :, col], preferred_element_type=jnp.float32)
+        u = u + jnp.dot(x0, wup[1, :, col], preferred_element_type=jnp.float32) + bias[...]
+        u = jnp.concatenate([jnp.where(second > 0, u[:slots], 0.0), u[slots:]], axis=0)
+        up[r] = u[slots:]
+        act[r] = snake(u, turns1, inv1).astype(jnp.bfloat16)
+        return carry
+
+    lax.fori_loop(0, stride, first, 0)
+
+    def tap(r, back):
+        s = r - back
+        same = s >= 0
+        which = jnp.where(same, s, s + stride)
+        start = pl.multiple_of(jnp.where(same, slots, 0), slots)
+        return act[which, pl.ds(start, live), :]
+
+    def second_half(r, carry):
+        d = jnp.dot(tap(r, 0), dw[0], preferred_element_type=jnp.float32)
+        d = d + jnp.dot(tap(r, DILATION_RATE), dw[1], preferred_element_type=jnp.float32)
+        d = d + jnp.dot(tap(r, 2 * DILATION_RATE), dw[2], preferred_element_type=jnp.float32)
+        b = snake(d, turns2, inv2).astype(jnp.bfloat16)
+        o = up[r] + jnp.dot(b, pw[...], preferred_element_type=jnp.float32)
+        for t in range(frames - 2):
+            piece = jnp.where(count > t, o[t * slots : (t + 1) * slots], 0.0)
+            at = pl.ds(t * stride + r, slots, stride=span)
+            out32[0, at, :] = piece[:, :half]
+            out32[1, at, :] = piece[:, half:]
+        return carry
+
+    lax.fori_loop(0, stride, second_half, 0)
+
+    def pack(s, carry):
+        at = pl.ds(pl.multiple_of(s * span, span), span)
+        out_ref[s] = jnp.concatenate([out32[0, at, :], out32[1, at, :]], axis=1).astype(
+            out_ref.dtype
         )
-        dilated_output = dilated_output + jnp.einsum(
-            "fgo,op->fgp",
-            kernel_tap_input,
-            dilated_weight[kernel_tap_index],
-            preferred_element_type=jnp.float32,
-        )
-    second_act = snake_act(dilated_output, snake_alpha_second).astype(jnp.bfloat16)
-    pointwise = jnp.einsum(
-        "fgo,op->fgp", second_act, pointwise_weight, preferred_element_type=jnp.float32
-    )
-    kept_mask = jnp.repeat(item_active_mask[:, CTX:], stride_len, axis=1)
-    return jnp.where(kept_mask[:, :, None], upsampled[:, output_start:] + pointwise, 0.0).astype(
-        jnp.bfloat16
-    )
+        return carry
+
+    lax.fori_loop(0, slots, pack, 0)
+
+
+def vocoder_kernel(slots, frames, stride, tab, x, wup, bias, a1, dw, a2, pw, out, up, act, out32):
+    vocode(
+        slots, frames, stride, lambda s: tab[s],
+        x, wup, bias, a1, dw, a2, pw, out, up, act, out32,
+    )
+
+
+def vocoder(tab, x, wup, bias, a1, dw, a2, pw, slots, frames, stride):
+    rows, width = x.shape[0], bias.shape[0]
+    span = (frames - 2) * stride
+    vmem = pl.BlockSpec(memory_space=pltpu.VMEM)
+    return pl.pallas_call(
+        functools.partial(vocoder_kernel, slots, frames, stride),
+        out_shape=jax.ShapeDtypeStruct((slots, span, width), jnp.bfloat16),
+        in_specs=[pl.BlockSpec(memory_space=pltpu.SMEM)] + [vmem] * 7,
+        out_specs=vmem,
+        scratch_shapes=[
+            pltpu.VMEM((stride, rows - 2 * slots, width), jnp.float32),
+            pltpu.VMEM((stride, rows - slots, width), jnp.bfloat16),
+            pltpu.VMEM((2, slots * span, width // 2), jnp.float32),
+        ],
+        compiler_params=pltpu.CompilerParams(vmem_limit_bytes=48 * 2**20),
+    )(tab, x, wup, bias[None], a1[None], dw, a2[None], pw)
 
 
 def body(
@@ -150,18 +208,14 @@
     arrived = lax.all_to_all(outgoing, "mp", split_axis=0, concat_axis=0, tiled=True)
     arrived = arrived.reshape(peer_count * send_cap, frames_item, latent_width)
     slot_entries = arrived[fetch_index]
-    slot_active_mask = (
-        item_active_mask.reshape(item_total, frames_item)[chosen_item] & present[:, None]
-    )
-    unit_output = vocoder_forward(
-        slot_entries,
-        slot_active_mask,
-        upsample_weight,
-        upsample_bias,
-        snake_alpha_first,
-        dilated_weight,
-        snake_alpha_second,
-        pointwise_weight,
+    chosen_count = stretch_frame_count.reshape(-1)[chosen_item]
+    tab = jnp.where(present, 1 + chosen_count * 2 + chosen_item * 256, 0).astype(jnp.int32)
+    stride_len = upsample_weight.shape[2] // up_width
+    wup = lax.all_gather(upsample_weight, "dp", axis=1, tiled=True)
+    x = jnp.transpose(slot_entries, (1, 0, 2)).reshape(frames_item * recv_cap, latent_width)
+    unit_output = vocoder(
+        tab, x, wup, upsample_bias, snake_alpha_first, dilated_weight,
+        snake_alpha_second, pointwise_weight, recv_cap, frames_item, stride_len,
     )
     return unit_output.reshape(1, recv_cap, 1, samples, up_width)
 

time: 158 us -> 142 us (0.90)
  matrix products: 20.4 us -> 2.65 us
  Pallas kernels: 0 us -> 9.47 us
  other arithmetic: 9.54 us -> 1.87 us
    dot_general x5 -> x0, matrix products: 17.8 us -> none  [the longest x1 8.96 us: vocoder_forward(): jnp.einsum('fgo,op->fgp', second_act, pointwise_weight, preferred_element...]
    pallas_call x0 -> x1, Pallas kernels: none -> 9.47 us  [vocoder(): pl.pallas_call(functools.partial(vocoder_kernel, slots, frames, stride),...]
    convert_element_type x2 -> x0, other arithmetic: 7.65 us -> none  [the longest x1 7.58 us: vocoder_forward(): snake_act(upsampled, snake_alpha_first).astype(jnp.bfloat16)]
    unnamed x24 -> x23, local copies, waits for them, and re-layouts: 0.71 us -> 2.57 us
    reshape x4 -> x1, local copies, waits for them, and re-layouts: 1.8 us -> 0.14 us  [body(): chosen_count = stretch_frame_count.reshape(-1)[chosen_item]]
  transfers between devices with their start and end apart: 3 -> 3, of which waited for: 2 -> 2; matrix products, arithmetic and copies ran while one was open for 5% -> 6% of each run, Pallas kernels for 0% -> 0%
where the time goes in v1:
time: 142 us; the launch traced here: 141 us
  waiting for transfers between devices  83.6 us (59%)
  between operations  15.1 us (11%)
  blocking collectives  13.3 us (9%)
  Pallas kernels  9.47 us (7%)
  local copies, waits for them, and re-layouts  8.33 us (6%)
  starting transfers between devices  7.12 us (5%)
  matrix products  2.65 us (2%)
  other arithmetic  1.87 us (1%)
    reduce_scatter x1, waiting for transfers between devices, body(): lax.psum_scatter(jnp.dot(hidden, head_weight, preferred_element_type=jnp....  66.4 us
    all_to_all x1, waiting for transfers between devices, body(): lax.all_to_all(outgoing, 'mp', split_axis=0, concat_axis=0, tiled=True)  16.6 us
    all_gather x1, blocking collectives, body(): head_weight = lax.all_gather(latent_head_weight, 'dp', axis=1, tiled=True)  13.3 us
    pallas_call x1, Pallas kernels, vocoder(): pl.pallas_call(functools.partial(vocoder_kernel, slots, frames, stride),...  9.47 us
    all_to_all x1, starting transfers between devices, body(): lax.all_to_all(outgoing, 'mp', split_axis=0, concat_axis=0, tiled=True)  7.07 us
  transfers between devices with their start and end apart: 3, of which 2 were waited for; matrix products, arithmetic and copies ran while one was open for 6% of the time, Pallas kernels for 0%

profile of v1, /device:TPU:1, one launch (start us, length us, event | category | flops | bytes accessed | tf_op | source)
XLA Modules:
  0.0 141.3 jit_solution(1407571770159761222)
XLA Ops:
  7.4 0.0 copy-start
  7.4 0.0 reduce-scatter.2.cloned.1.call-start
  7.4 13.3 %all_gather.6 = bf16[512,512]{1,0:T(8,128)(2,1)S(1)} all-gather(bf16[512,128]{1,0:T(8,128)(2,1)} %param.12), channel_id=1, replica_groups=mesh['pipe'=8,'mp'=16,'dp'=4] {'dp'}, dimensions={1}, use_global_device_ids=true | all-gather | bytes 655360 | tf_op jit(solution)/shard_map/all_gather | solution.py:156
  20.6 0.0 copy-done
  20.6 2.7 %fusion.9 = f32[1536,512]{1,0:T(8,128)} fusion(bf16[1536,512]{1,0:T(8,128)(2,1)S(1)} %copy-done, bf16[512,512]{1,0:T(8,128)(2,1)S(1)} %all_gather.6), kind=kOutput, calls=%fused_computation.47 | convolution fusion | flops 805306368 | bytes 5242880 | tf_op jit(solution)/shard_map/dot_general | solution.py:159
  23.3 0.0 copy-start.7
  23.3 0.0 copy-start.8
  23.3 0.0 copy-start.9
  23.3 0.0 reduce-scatter.2.cloned.1.call-update
  23.3 0.0 all-gather.2.cloned.1.call-start
  23.4 0.5 all-gather.2.cloned.1.call-update
  23.9 0.1 copy-done.7
  24.0 0.1 copy.33
  24.1 0.1 compare_and_fusion
  24.2 0.1 dynamic-slice_add_fusion
  24.3 0.1 copy.34
  24.4 0.1 add_select_fusion
  24.5 0.1 broadcast_in_dim.71.clone
  24.6 0.1 fusion.1
  24.7 0.1 copy.37
  24.8 0.1 broadcast_in_dim_reshape.14
  24.9 0.1 reshape.421
  25.0 0.0 copy-done.8
  25.0 0.1 copy.31
  25.1 0.1 broadcast_in_dim_reshape.12
  25.2 0.0 copy-done.9
  25.2 0.1 copy.32
  25.3 0.1 eq.54
  25.5 0.1 reshape.399
  25.6 0.2 convert_reduce_fusion
  25.8 0.1 compare_select_fusion.3
  25.9 0.1 select_reduce_fusion
  26.0 66.4 %reduce-scatter.2.cloned.1.call-done = f32[96,512]{1,0:T(8,128)} async-done(((f32[1536,512]{1,0:T(8,128)}), f32[96,512]{1,0:T(8,128)}) %reduce-scatter.2.cloned.1.call-update) | async-done | bytes 196624 | tf_op jit(solution)/shard_map/reduce_scatter | solution.py:158
  92.4 0.9 convert_element_type.11
  93.4 1.7 %gather_fusion.2 = bf16[112,512]{1,0:T(8,128)(2,1)S(1)} fusion(bf16[4,24,512]{2,1,0:T(8,128)(2,1)S(1)} %bitcast.30, s32[112]{0:T(128)S(1)} %reshape.421), kind=kCustom, calls=%fused_computation.2 | custom fusion | bytes 230272 | tf_op jit(solution)/shard_map/jit(take_along_axis)/gather | solution.py:178
  95.1 0.1 select_select_fusion
  95.2 0.1 broadcast_in_dim.68
  95.3 0.7 scatter_fusion
  96.0 0.9 reshape.401
  96.9 0.0 copy-start.2
  96.9 0.0 copy-start.3
  96.9 0.0 copy-start.4
  96.9 0.0 copy-start.5
  96.9 0.0 copy-start.6
  96.9 7.1 %all-to-all-start = ((bf16[16,28,512]{2,1,0:T(8,128)(2,1)}), bf16[16,28,512]{2,1,0:T(8,128)(2,1)S(1)}, u32[]{:S(2)}, u32[]{:S(2)}) async-start(bf16[16,28,512]{2,1,0:T(8,128)(2,1)} %reshape.401), calls=%async_computation.1 | async-start | bytes 1048576 | tf_op jit(solution)/shard_map/all_to_all | solution.py:208
  104.0 0.7 gather_fusion
  104.7 16.6 %all-to-all-done = bf16[16,28,512]{2,1,0:T(8,128)(2,1)S(1)} async-done(((bf16[16,28,512]{2,1,0:T(8,128)(2,1)}), bf16[16,28,512]{2,1,0:T(8,128)(2,1)S(1)}, u32[]{:S(2)}, u32[]{:S(2)}) %all-to-all-start) | async-done | bytes 458784 | tf_op jit(solution)/shard_map/all_to_all | solution.py:208
  121.3 0.1 reshape.402
  121.4 0.6 gather_fusion.1
  122.0 0.1 copy.39
  122.1 0.0 all-gather.2.cloned.1.call-done.wup
  122.2 0.0 copy-done.2
  122.2 0.0 copy-done.3
  122.2 0.0 copy-done.4
  122.2 0.0 copy-done.5
  122.2 0.0 copy-done.6
  122.2 0.0 copy-start.1
  122.2 2.2 %copy-done.1 = bf16[2,512,2048]{2,1,0:T(8,128)(2,1)S(1)} copy-done((bf16[2,512,2048]{2,1,0:T(8,128)(2,1)S(1)}, bf16[2,512,2048]{2,1,0:T(8,128)(2,1)}, u32[]{:S(2)}) %copy-start.1) | copy-done | bytes 4194328
  124.4 9.5 %shard_map.109 = bf16[16,96,256]{2,1,0:T(8,128)(2,1)} custom-call(s32[16]{0:T(128)S(1)} %compare_select_fusion.5.tab, bf16[224,512]{1,0:T(8,128)(2,1)S(1)} %bitcast.26, bf16[2,512,2048]{2,1,0:T(8,128)(2,1)S(1)} %copy-done.1, f32[1,256]{1,0:T(1,128)S(1)} %bitcast.27, f32[1,256]{1,0:T(1,128)S(1)} %bitcast.28, bf16[3,256,256]{2,1,0:T(8,128)(2,1)S(1)} %copy-done.2, ...), custom_call_target="tpu_custom_call" | custom-call | tf_op jit(solution)/shard_map/pallas_call | solution.py:127
  (16 shorter events, 0.1 us)
Async XLA Ops:
  7.4 13.3 %copy-start = (bf16[1536,512]{1,0:T(8,128)(2,1)S(1)}, bf16[1536,512]{1,0:T(8,128)(2,1)}, u32[]{:S(2)}) copy-start(bf16[1536,512]{1,0:T(8,128)(2,1)} %param.11) | copy-start | bytes 4718596
  7.4 85.1 %reduce-scatter.2.cloned.1.call-start = ((), (), s32[]{:S(2)}) async-start(), calls=%async_computation.2 | async-start | bytes 3342336 | tf_op jit(solution)/shard_map/reduce_scatter | solution.py:158
  23.3 0.7 copy-start.7
  23.3 1.7 %copy-start.8 = (s32[64,2]{0,1:T(2,128)S(1)}, s32[64,2]{0,1:T(2,128)}, u32[]{:S(2)}) copy-start(s32[64,2]{0,1:T(2,128)} %param.13) | copy-start | bytes 1540
  23.3 1.9 %copy-start.9 = (s32[64,2]{0,1:T(2,128)S(1)}, s32[64,2]{0,1:T(2,128)}, u32[]{:S(2)}) copy-start(s32[64,2]{0,1:T(2,128)} %param.14) | copy-start | bytes 1540
  23.3 98.8 %all-gather.2.cloned.1.call-start = ((), (), s32[]{:S(2)}) async-start(), calls=%async_computation.3 | async-start | bytes 5242880 | tf_op jit(solution)/shard_map/all_gather | solution.py:214
  96.9 25.3 %copy-start.2 = (bf16[3,256,256]{2,1,0:T(8,128)(2,1)S(1)}, bf16[3,256,256]{2,1,0:T(8,128)(2,1)}, u32[]{:S(2)}) copy-start(bf16[3,256,256]{2,1,0:T(8,128)(2,1)} %dw.1) | copy-start | bytes 1179652
  96.9 25.3 %copy-start.3 = (bf16[256,256]{1,0:T(8,128)(2,1)S(1)}, bf16[256,256]{1,0:T(8,128)(2,1)}, u32[]{:S(2)}) copy-start(bf16[256,256]{1,0:T(8,128)(2,1)} %pw.1) | copy-start | bytes 393220
  96.9 25.3 %copy-start.4 = (f32[256]{0:T(256)S(1)}, f32[256]{0:T(256)}, u32[]{:S(2)}) copy-start(f32[256]{0:T(256)} %param.17) | copy-start | bytes 3076
  96.9 25.3 %copy-start.5 = (f32[256]{0:T(256)S(1)}, f32[256]{0:T(256)}, u32[]{:S(2)}) copy-start(f32[256]{0:T(256)} %param.18) | copy-start | bytes 3076
  96.9 25.3 %copy-start.6 = (f32[256]{0:T(256)S(1)}, f32[256]{0:T(256)}, u32[]{:S(2)}) copy-start(f32[256]{0:T(256)} %param.20) | copy-start | bytes 3076
  96.9 24.4 %all-to-all-start = ((bf16[16,28,512]{2,1,0:T(8,128)(2,1)}), bf16[16,28,512]{2,1,0:T(8,128)(2,1)S(1)}, u32[]{:S(2)}, u32[]{:S(2)}) async-start(bf16[16,28,512]{2,1,0:T(8,128)(2,1)} %reshape.401), calls=%async_computation.1 | async-start | bytes 1048576 | tf_op jit(solution)/shard_map/all_to_all | solution.py:208
  122.2 2.2 %copy-start.1 = (bf16[2,512,2048]{2,1,0:T(8,128)(2,1)S(1)}, bf16[2,512,2048]{2,1,0:T(8,128)(2,1)}, u32[]{:S(2)}) copy-start(bf16[2,512,2048]{2,1,0:T(8,128)(2,1)} %all-gather.2.cloned.1.call-done.wup) | copy-start | bytes 12582916
Sparse Core Ops, SparseCore 0:
  23.4 68.9 reduce-scatter.1
Sparse Core Ops, SparseCore 1:
  25.9 59.2 all-gather.1

commit v2 on v1

v2 whole, which is shorter than its diff:
```python
import functools

import jax
import jax.numpy as jnp
from jax import lax
from jax.experimental import pallas as pl
from jax.experimental.pallas import tpu as pltpu
from jax.sharding import PartitionSpec as P

DILATION_RATE = 3
CTX = 2
TILE = 16
BLOCKS = 4
MESH = pl.DeviceIdType.MESH

SIN2 = (
    9.869604110717773,
    -32.469669342041016,
    42.727195739746094,
    -30.101465225219727,
    13.05009937286377,
    -3.3565926551818848,
)


def snake(v, turns, inverse):
    u = v * turns
    r = u - jnp.round(u)
    s = r * r
    q = jnp.full_like(s, SIN2[-1])
    for c in SIN2[-2::-1]:
        q = q * s + c
    return v + (q * s) * inverse


def vocode(slots, frames, stride, tab, x_ref, wup, bias, a1, dw, a2, pw, out_ref, up, act, out32):
    rows = frames * slots
    live = rows - CTX * slots
    width = bias.shape[1]
    half = width // 2
    span = (frames - CTX) * stride
    lane = lax.broadcasted_iota(jnp.int32, (slots, width), 0)
    count = jnp.zeros((slots, width), jnp.int32)
    second = jnp.zeros((slots, width), jnp.int32)
    for s in range(slots):
        word = tab(s)
        count = jnp.where(lane == s, (word // 2) % 16, count)
        second = jnp.where(lane == s, (word // 256) % 2, second)
    turns1 = a1[...] * (1.0 / jnp.pi)
    inv1 = 1.0 / a1[...]
    turns2 = a2[...] * (1.0 / jnp.pi)
    inv2 = 1.0 / a2[...]
    x1 = x_ref[pl.ds(slots, rows - slots), :]
    x0 = x_ref[pl.ds(0, rows - slots), :]

    def first(r, carry):
        col = pl.ds(pl.multiple_of(r * width, width), width)
        u = jnp.dot(x1, wup[0, :, col], preferred_element_type=jnp.float32)
        u = u + jnp.dot(x0, wup[1, :, col], preferred_element_type=jnp.float32) + bias[...]
        u = jnp.concatenate([jnp.where(second > 0, u[:slots], 0.0), u[slots:]], axis=0)
        up[r] = u[slots:]
        act[r] = snake(u, turns1, inv1).astype(jnp.bfloat16)
        return carry

    lax.fori_loop(0, stride, first, 0)

    def tap(r, back):
        s = r - back
        same = s >= 0
        which = jnp.where(same, s, s + stride)
        start = pl.multiple_of(jnp.where(same, slots, 0), slots)
        return act[which, pl.ds(start, live), :]

    def second_half(r, carry):
        d = jnp.dot(tap(r, 0), dw[0], preferred_element_type=jnp.float32)
        d = d + jnp.dot(tap(r, DILATION_RATE), dw[1], preferred_element_type=jnp.float32)
        d = d + jnp.dot(tap(r, 2 * DILATION_RATE), dw[2], preferred_element_type=jnp.float32)
        b = snake(d, turns2, inv2).astype(jnp.bfloat16)
        o = up[r] + jnp.dot(b, pw[...], preferred_element_type=jnp.float32)
        for t in range(frames - CTX):
            piece = jnp.where(count > t, o[t * slots : (t + 1) * slots], 0.0)
            at = pl.ds(t * stride + r, slots, stride=span)
            out32[0, at, :] = piece[:, :half]
            out32[1, at, :] = piece[:, half:]
        return carry

    lax.fori_loop(0, stride, second_half, 0)

    def pack(s, carry):
        at = pl.ds(pl.multiple_of(s * span, span), span)
        out_ref[s] = jnp.concatenate([out32[0, at, :], out32[1, at, :]], axis=1).astype(
            out_ref.dtype
        )
        return carry

    lax.fori_loop(0, slots, pack, 0)


def kernel(
    slots, frames, stride, n_z, n_y, n_x,
    tab, src, hidden, head, wupin, bias, a1, dw, a2, pw,
    out,
    hid, hpad, tiles, hperm, hw, pbuf, sib, rx0, rx, tx0, tx, x, wup, up, act, out32,
    local_sem, head_s, head_r, pair_s, pair_r, ring_s, ring_r, upx_s, upx_r, upz_s, upz_r, upc_s, upc_r,
):
    zi, mi, xi = lax.axis_index("pipe"), lax.axis_index("mp"), lax.axis_index("dp")
    y, c = lax.div(mi, 2), lax.rem(mi, 2)
    rows = frames * slots
    mid = rows // 2
    cols = head.shape[1]

    def peer(dz=0, dy=0, dc=0, dx=0):
        return (
            lax.rem(zi + dz + n_z, n_z),
            lax.rem(y + dy + n_y, n_y) * 2 + lax.rem(c + dc, 2),
            lax.rem(xi + dx + n_x, n_x),
        )

    sibling = peer(dc=1)
    ring = (peer(dy=1), peer(dy=-1))
    across = (peer(dx=1), peer(dx=-1), peer(dx=2))
    origin = (lax.rem(xi + n_x - 1, n_x), lax.rem(xi + 1, n_x), lax.rem(xi + 2, n_x))
    updown = (peer(dz=1), peer(dz=-1))
    sent = []

    def remote(src_ref, dst_ref, s, r, to):
        return pltpu.make_async_remote_copy(
            src_ref=src_ref, dst_ref=dst_ref, send_sem=s, recv_sem=r, device_id=to, device_id_type=MESH
        )

    def send(*a):
        copy = remote(*a)
        copy.start()
        sent.append(copy)

    def arrived(ref, s, r):
        remote(ref, ref, s, r, sibling).wait_recv()

    load = pltpu.make_async_copy(hidden, hid, local_sem.at[0])
    load.start()
    piece = wupin.shape[1]
    own_up = pltpu.make_async_copy(
        wupin, wup.at[:, pl.ds(pl.multiple_of(xi * piece, piece), piece), :], local_sem.at[1]
    )
    own_up.start()
    barrier = pltpu.get_barrier_semaphore()
    for other in (sibling, *ring, *across, *updown):
        pl.semaphore_signal(barrier, inc=1, device_id=other, device_id_type=MESH)
    load.wait()

    n_groups, per = src.shape
    rows_in = hid.shape[0] // n_groups
    tiles_in = per // TILE

    def pad(g, carry):
        row = lax.broadcasted_iota(jnp.int32, (rows_in, per), 0)
        pick = jnp.where(row == src[pl.ds(g, 1), :], 1.0, 0.0).astype(jnp.bfloat16)
        h = hid[pl.ds(pl.multiple_of(g * rows_in, rows_in), rows_in), :]
        got = lax.dot_general(
            pick, h, (((0,), (0,)), ((), ())), preferred_element_type=jnp.float32
        ).astype(jnp.bfloat16)
        hpad[pl.ds(g * tiles_in, tiles_in)] = got.reshape(tiles_in, TILE, got.shape[1])
        return carry

    lax.fori_loop(0, n_groups, pad, 0)

    i = lax.broadcasted_iota(jnp.int32, (rows, slots * TILE), 0)
    j = lax.broadcasted_iota(jnp.int32, (rows, slots * TILE), 1)
    turn = jnp.where((i % slots) * TILE + i // slots == j, 1.0, 0.0).astype(jnp.bfloat16)

    def gather(n, carry):
        part, k = lax.div(n, n_y), lax.rem(n, n_y)
        owner = lax.rem(y + k, n_y) * 2 + lax.rem(c + 1 + part, 2)
        for s in range(slots):
            item = tab[owner * slots + s] // 256
            tiles[s * TILE : (s + 1) * TILE, :] = hpad[item]
        hperm[part, k] = jnp.dot(turn, tiles[...], preferred_element_type=jnp.float32).astype(
            jnp.bfloat16
        )
        return carry

    lax.fori_loop(0, 2 * n_y, gather, 0)

    def project(b, part):
        def one(k, carry):
            w = head[...] if b == 0 else hw[b - 1]
            pbuf[b, part, k] = jnp.dot(
                hperm[part, k], w, preferred_element_type=jnp.float32
            ).astype(jnp.bfloat16)
            return carry

        lax.fori_loop(0, n_y, one, 0)

    project(0, 0)
    project(0, 1)
    pl.semaphore_wait(barrier, 8)

    def pair(b):
        send(pbuf.at[b, 0], sib.at[b], pair_s.at[b], pair_r.at[b], sibling)

    def own(b, k):
        return pbuf[b, 1, k].astype(jnp.float32) + sib[b, k].astype(jnp.float32)

    def step(b, s):
        if s == 0:
            arrived(sib.at[b], pair_s.at[b], pair_r.at[b])
            v = own(b, n_y // 2).astype(jnp.bfloat16)
            tx0[b, 0] = v[:mid]
            tx0[b, 1] = v[mid:]
            for d in range(2):
                send(tx0.at[b, d], rx0.at[b, d], ring_s.at[b, d, 0], ring_r.at[b, d, 0], ring[d])
            return
        for d in range(2):
            k = n_y // 2 - s if d == 0 else n_y // 2 + s
            v = own(b, k)
            if s == 1:
                arrived(rx0.at[b, d], ring_s.at[b, d, 0], ring_r.at[b, d, 0])
                more = rx0[b, d].astype(jnp.float32)
                if d == 0:
                    v = jnp.concatenate([v[:mid] + more, v[mid:]], axis=0)
                else:
                    v = jnp.concatenate([v[:mid], v[mid:] + more], axis=0)
            else:
                arrived(rx.at[b, d, s - 2], ring_s.at[b, d, s - 1], ring_r.at[b, d, s - 1])
                v = v + rx[b, d, s - 2].astype(jnp.float32)
            tx[b, d, s - 1] = v.astype(jnp.bfloat16)
            send(tx.at[b, d, s - 1], rx.at[b, d, s - 1], ring_s.at[b, d, s], ring_r.at[b, d, s], ring[d])

    def final(b):
        v = own(b, 0)
        last = n_y // 2 - 1
        for d in range(2):
            arrived(rx.at[b, d, last - 1], ring_s.at[b, d, last], ring_r.at[b, d, last])
            v = v + rx[b, d, last - 1].astype(jnp.float32)
        q = xi if b == 0 else origin[b - 1]
        x[:, pl.ds(pl.multiple_of(q * cols, cols), cols)] = v.astype(jnp.bfloat16)

    def head_in(j):
        arrived(hw.at[j], head_s.at[j], head_r.at[j])
        project(j + 1, 0)
        pair(j + 1)
        project(j + 1, 1)

    half, quarter = piece // 2, piece // 4
    e = lax.rem(zi, 2)

    def up_rows(q, offset, n):
        return wup.at[:, pl.ds(pl.multiple_of(q * piece + offset, n), n), :]

    def upx_send():
        mine = wupin.at[:, pl.ds(pl.multiple_of(c * half + e * quarter, quarter), quarter), :]
        for j in range(3):
            send(mine, up_rows(xi, c * half + e * quarter, quarter), upx_s.at[j], upx_r.at[j], across[j])

    def upx_in(j):
        at = c * half + e * quarter
        arrived(up_rows(origin[j], at, quarter), upx_s.at[j], upx_r.at[j])
        for d in range(2):
            ref = up_rows(origin[j], at + d * (quarter // 2), quarter // 2)
            send(ref, ref, upz_s.at[j, d], upz_r.at[j, d], updown[d])

    def upz_in(j):
        at = c * half + (1 - e) * quarter
        for d in range(2):
            ref = up_rows(origin[j], at + d * (quarter // 2), quarter // 2)
            arrived(ref, upz_s.at[j, d], upz_r.at[j, d])
        ref = up_rows(origin[j], c * half, half)
        send(ref, ref, upc_s.at[j], upc_r.at[j], sibling)

    def upc_in(j):
        arrived(up_rows(origin[j], (1 - c) * half, half), upc_s.at[j], upc_r.at[j])

    for j in range(3):
        send(head, hw.at[j], head_s.at[j], head_r.at[j], across[j])
    pair(0)
    step(0, 0)
    head_in(0)
    head_in(1)
    upx_send()
    step(0, 1)
    step(1, 0)
    head_in(2)
    step(2, 0)
    step(0, 2)
    step(1, 1)
    step(3, 0)
    step(2, 1)
    step(0, 3)
    step(1, 2)
    step(3, 1)
    step(2, 2)
    final(0)
    upx_in(0)
    step(1, 3)
    step(3, 2)
    step(2, 3)
    upx_in(1)
    final(1)
    step(3, 3)
    upx_in(2)
    upz_in(0)
    upz_in(1)
    final(2)
    upz_in(2)
    final(3)
    for j in range(3):
        upc_in(j)
    own_up.wait()
    for copy in sent:
        copy.wait_send()
    vocode(
        slots, frames, stride, lambda s: tab[mi * slots + s],
        x, wup, bias, a1, dw, a2, pw, out, up, act, out32,
    )


def body(
    hidden,
    latent_head_weight,
    stretch_holder,
    stretch_position,
    stretch_frame_count,
    upsample_weight,
    upsample_bias,
    snake_alpha_first,
    dilated_weight,
    snake_alpha_second,
    pointwise_weight,
):
    n_z, n_mp, n_x = lax.axis_size("pipe"), lax.axis_size("mp"), lax.axis_size("dp")
    n_y = n_mp // 2
    streams = stretch_frame_count.shape[0]
    items = 2 * streams
    seq_len = hidden.shape[0] // streams
    stretch_len = seq_len // 2
    slots = 2 * items // n_mp
    frames = stretch_len + CTX
    rows = frames * slots
    width = upsample_bias.shape[0]
    stride = upsample_weight.shape[2] // width
    span = stretch_len * stride
    depth, cols = latent_head_weight.shape
    latent = cols * n_x

    item = jnp.arange(items, dtype=jnp.int32).reshape(streams, 2)
    key = stretch_holder * slots + stretch_position
    word = 1 + 2 * stretch_frame_count + 256 * item
    place = jnp.arange(n_mp * slots, dtype=jnp.int32)
    tab = jnp.sum(jnp.where(key[:, :, None] == place, word[:, :, None], 0), axis=(0, 1))
    group = TILE // 2
    j = jnp.arange(TILE, dtype=jnp.int32)[None, None, :]
    st = (item % TILE)[:, :, None]
    back = stretch_frame_count[:, 0:1, None] - CTX + j
    back = jnp.where((item[:, :, None] % 2 == 1) & (back >= 0), (st // 2) * seq_len + back, -1)
    here = jnp.where(j < frames, st * stretch_len + j - CTX, -1)
    src = jnp.where(j < CTX, back, here).reshape(streams // group, 2 * group * TILE)

    vmem = pl.BlockSpec(memory_space=pltpu.VMEM)
    anywhere = pl.BlockSpec(memory_space=pl.ANY)
    bf16, f32 = jnp.bfloat16, jnp.float32
    dma = pltpu.SemaphoreType.DMA
    out = pl.pallas_call(
        functools.partial(kernel, slots, frames, stride, n_z, n_y, n_x),
        out_shape=jax.ShapeDtypeStruct((slots, span, width), bf16),
        in_specs=[pl.BlockSpec(memory_space=pltpu.SMEM), vmem, anywhere, vmem, anywhere] + [vmem] * 5,
        out_specs=vmem,
        scratch_shapes=[
            pltpu.VMEM(hidden.shape, bf16),
            pltpu.VMEM((items, TILE, depth), bf16),
            pltpu.VMEM((slots * TILE, depth), bf16),
            pltpu.VMEM((2, n_y, rows, depth), bf16),
            pltpu.VMEM((3, depth, cols), bf16),
            pltpu.VMEM((BLOCKS, 2, n_y, rows, cols), bf16),
            pltpu.VMEM((BLOCKS, n_y, rows, cols), bf16),
            pltpu.VMEM((BLOCKS, 2, rows // 2, cols), bf16),
            pltpu.VMEM((BLOCKS, 2, 3, rows, cols), bf16),
            pltpu.VMEM((BLOCKS, 2, rows // 2, cols), bf16),
            pltpu.VMEM((BLOCKS, 2, 3, rows, cols), bf16),
            pltpu.VMEM((rows, latent), bf16),
            pltpu.VMEM((2, latent, stride * width), bf16),
            pltpu.VMEM((stride, rows - CTX * slots, width), f32),
            pltpu.VMEM((stride, rows - slots, width), bf16),
            pltpu.VMEM((2, slots * span, width // 2), f32),
            dma((2,)),
            dma((3,)), dma((3,)),
            dma((BLOCKS,)), dma((BLOCKS,)),
            dma((BLOCKS, 2, 4)), dma((BLOCKS, 2, 4)),
            dma((3,)), dma((3,)),
            dma((3, 2)), dma((3, 2)),
            dma((3,)), dma((3,)),
        ],
        compiler_params=pltpu.CompilerParams(
            collective_id=0, has_side_effects=True, vmem_limit_bytes=56 * 2**20
        ),
    )(
        tab, src, hidden, latent_head_weight, upsample_weight,
        upsample_bias[None], snake_alpha_first[None], dilated_weight,
        snake_alpha_second[None], pointwise_weight,
    )
    return out.reshape(1, slots, 1, span, width)


def solution(mesh):
    in_specs = (
        P(("pipe", "dp"), "mp"),
        P("mp", "dp"),
        P(("pipe", "dp"), None),
        P(("pipe", "dp"), None),
        P(("pipe", "dp"), None),
        P(None, "dp", None),
        P(),
        P(),
        P(),
        P(),
        P(),
    )
    out_specs = P("pipe", "mp", "dp", None, None)
    return jax.shard_map(body, mesh=mesh, in_specs=in_specs, out_specs=out_specs, check_vma=False)
```

time: 142 us -> 78 us (0.55)
  waiting for transfers between devices: 83.6 us -> 0 us
  Pallas kernels: 9.47 us -> 72 us
  between operations: 15.1 us -> 0.04 us
  blocking collectives: 13.3 us -> 0 us
  starting transfers between devices: 7.12 us -> 0 us
  local copies, waits for them, and re-layouts: 8.33 us -> 3.1 us
  matrix products: 2.65 us -> 0 us
    reduce_scatter x1 -> x0, waiting for transfers between devices: 66.4 us -> none  [body(): lax.psum_scatter(jnp.dot(hidden, head_weight, preferred_element_type=jnp....]
    pallas_call x1, Pallas kernels: 9.47 us -> 72 us  [body(): pl.pallas_call(functools.partial(kernel, slots, frames, stride, n_z, n_y,...]
    all_to_all x1 -> x0, waiting for transfers between devices: 16.6 us -> none  [body(): lax.all_to_all(outgoing, 'mp', split_axis=0, concat_axis=0, tiled=True)]
    all_gather x1 -> x0, blocking collectives: 13.3 us -> none  [body(): head_weight = lax.all_gather(latent_head_weight, 'dp', axis=1, tiled=True)]
    all_to_all x1 -> x0, starting transfers between devices: 7.07 us -> none  [body(): lax.all_to_all(outgoing, 'mp', split_axis=0, concat_axis=0, tiled=True)]
    gather x5 -> x0, local copies, waits for them, and re-layouts: 3 us -> none  [the longest x3 1.78 us: body(): picked = jnp.take_along_axis(stream_latent, my_rows[:, :, None], axis=1)]
    dot_general x1 -> x0, matrix products: 2.65 us -> none  [body(): jnp.dot(hidden, head_weight, preferred_element_type=jnp.float32)]
  transfers between devices with their start and end apart: 3 -> 0, of which waited for: 2 -> 0; matrix products, arithmetic and copies ran while one was open for 6% -> 0% of each run, Pallas kernels for 0% -> 0%
where the time goes in v2:
time: 78 us; the launch traced here: 77.7 us
  Pallas kernels  72 us (92%)
  local copies, waits for them, and re-layouts  3.1 us (4%)
  other arithmetic  2.57 us (3%)
    pallas_call x1, Pallas kernels, body(): pl.pallas_call(functools.partial(kernel, slots, frames, stride, n_z, n_y,...  72 us
    unnamed x1, local copies, waits for them, and re-layouts  2.06 us

profile of v2, /device:TPU:1, one launch (start us, length us, event | category | flops | bytes accessed | tf_op | source)
XLA Modules:
  0.0 77.7 jit_solution(9588040214218903486)
XLA Ops:
  0.0 0.7 add_bitcast_fusion
  0.7 0.7 multiply_add_fusion
  1.5 0.7 select_reduce_fusion.tab
  2.2 0.1 copy.24
  2.3 0.1 broadcast_compare_fusion
  2.4 0.1 copy.25
  2.5 0.1 copy.26
  2.5 0.1 iota_add_fusion
  2.6 0.3 fusion
  2.9 0.7 select_n.68.src
  3.6 72.0 %shard_map.109 = bf16[16,96,256]{2,1,0:T(8,128)(2,1)} custom-call(s32[256]{0:T(256)} %select_reduce_fusion.tab, s32[8,256]{1,0:T(8,128)} %select_n.68.src, bf16[1536,512]{1,0:T(8,128)(2,1)} %hidden.1, bf16[512,128]{1,0:T(8,128)(2,1)} %head.1, bf16[2,128,2048]{2,1,0:T(8,128)(2,1)} %wupin.1, f32[1,256]{1,0:T(1,128)} %bitcast.9, f32[1,256]{1,0:T(1,128)} %bitcast.10, ...), custom_call_target="tpu_custom_call" | custom-call | tf_op jit(solution)/shard_map/pallas_call | solution.py:362
  75.6 2.1 %copy.29 = bf16[1,16,1,96,256]{4,3,2,1,0:T(8,128)(2,1)} copy(bf16[1,16,1,96,256]{4,3,2,1,0:T(8,128)(2,1)} %bitcast.8) | data formatting | bytes 1572864
  (4 shorter events, 0.1 us)

commit v3 on v2

--- a/solution.py
+++ b/solution.py
@@ -11,6 +11,7 @@
 CTX = 2
 TILE = 16
 BLOCKS = 4
+LOADS = 4
 MESH = pl.DeviceIdType.MESH
 
 SIN2 = (
@@ -33,19 +34,21 @@
     return v + (q * s) * inverse
 
 
-def vocode(slots, frames, stride, tab, x_ref, wup, bias, a1, dw, a2, pw, out_ref, up, act, out32):
+def twice(n, step, per=2):
+    def some(i, carry):
+        for j in range(per):
+            step(per * i + j, carry)
+        return carry
+
+    lax.fori_loop(0, n // per, some, 0)
+
+
+def vocode(slots, frames, stride, count, second, x_ref, wup, bias, a1, dw, a2, pw, out_ref, up, act, out32):
     rows = frames * slots
     live = rows - CTX * slots
     width = bias.shape[1]
     half = width // 2
     span = (frames - CTX) * stride
-    lane = lax.broadcasted_iota(jnp.int32, (slots, width), 0)
-    count = jnp.zeros((slots, width), jnp.int32)
-    second = jnp.zeros((slots, width), jnp.int32)
-    for s in range(slots):
-        word = tab(s)
-        count = jnp.where(lane == s, (word // 2) % 16, count)
-        second = jnp.where(lane == s, (word // 256) % 2, second)
     turns1 = a1[...] * (1.0 / jnp.pi)
     inv1 = 1.0 / a1[...]
     turns2 = a2[...] * (1.0 / jnp.pi)
@@ -57,12 +60,12 @@
         col = pl.ds(pl.multiple_of(r * width, width), width)
         u = jnp.dot(x1, wup[0, :, col], preferred_element_type=jnp.float32)
         u = u + jnp.dot(x0, wup[1, :, col], preferred_element_type=jnp.float32) + bias[...]
-        u = jnp.concatenate([jnp.where(second > 0, u[:slots], 0.0), u[slots:]], axis=0)
+        u = jnp.concatenate([jnp.where(second, u[:slots], 0.0), u[slots:]], axis=0)
         up[r] = u[slots:]
         act[r] = snake(u, turns1, inv1).astype(jnp.bfloat16)
         return carry
 
-    lax.fori_loop(0, stride, first, 0)
+    twice(stride, first)
 
     def tap(r, back):
         s = r - back
@@ -84,7 +87,7 @@
             out32[1, at, :] = piece[:, half:]
         return carry
 
-    lax.fori_loop(0, stride, second_half, 0)
+    twice(stride, second_half)
 
     def pack(s, carry):
         at = pl.ds(pl.multiple_of(s * span, span), span)
@@ -98,16 +101,16 @@
 
 def kernel(
     slots, frames, stride, n_z, n_y, n_x,
-    tab, src, hidden, head, wupin, bias, a1, dw, a2, pw,
+    holder, position, counts, bias, a1, a2, hidden, headin, wupin, dwin, pwin,
     out,
-    hid, hpad, tiles, hperm, hw, pbuf, sib, rx0, rx, tx0, tx, x, wup, up, act, out32,
+    hid, head, dw, pw, sel, pick, framed, hw2, hw1, pbuf, sib, rx0, rx, tx0, tx, x, wup, up, act, out32,
     local_sem, head_s, head_r, pair_s, pair_r, ring_s, ring_r, upx_s, upx_r, upz_s, upz_r, upc_s, upc_r,
 ):
     zi, mi, xi = lax.axis_index("pipe"), lax.axis_index("mp"), lax.axis_index("dp")
     y, c = lax.div(mi, 2), lax.rem(mi, 2)
     rows = frames * slots
     mid = rows // 2
-    cols = head.shape[1]
+    cols = headin.shape[1]
 
     def peer(dz=0, dy=0, dc=0, dx=0):
         return (
@@ -136,63 +139,114 @@
     def arrived(ref, s, r):
         remote(ref, ref, s, r, sibling).wait_recv()
 
-    load = pltpu.make_async_copy(hidden, hid, local_sem.at[0])
-    load.start()
+    streams = holder.shape[1]
+    items = 2 * streams
+    per = TILE // 2
+    groups = streams // per
+    seq = hid.shape[0] // streams
+    half_seq = seq // 2
+    rows_in = per * seq
+    chunk = hid.shape[0] // LOADS
+    loads = [
+        pltpu.make_async_copy(
+            hidden.at[pl.ds(n * chunk, chunk)], hid.at[pl.ds(n * chunk, chunk)], local_sem.at[n]
+        )
+        for n in range(LOADS)
+    ]
     piece = wupin.shape[1]
-    own_up = pltpu.make_async_copy(
-        wupin, wup.at[:, pl.ds(pl.multiple_of(xi * piece, piece), piece), :], local_sem.at[1]
-    )
-    own_up.start()
+    head_load = pltpu.make_async_copy(headin, head, local_sem.at[LOADS])
+    others = [
+        pltpu.make_async_copy(
+            wupin,
+            wup.at[:, pl.ds(pl.multiple_of(xi * piece, piece), piece), :],
+            local_sem.at[LOADS + 1],
+        ),
+        pltpu.make_async_copy(dwin, dw, local_sem.at[LOADS + 2]),
+        pltpu.make_async_copy(pwin, pw, local_sem.at[LOADS + 3]),
+    ]
+    for copy in (head_load, *loads, *others):
+        copy.start()
     barrier = pltpu.get_barrier_semaphore()
     for other in (sibling, *ring, *across, *updown):
         pl.semaphore_signal(barrier, inc=1, device_id=other, device_id_type=MESH)
-    load.wait()
-
-    n_groups, per = src.shape
-    rows_in = hid.shape[0] // n_groups
-    tiles_in = per // TILE
-
-    def pad(g, carry):
-        row = lax.broadcasted_iota(jnp.int32, (rows_in, per), 0)
-        pick = jnp.where(row == src[pl.ds(g, 1), :], 1.0, 0.0).astype(jnp.bfloat16)
-        h = hid[pl.ds(pl.multiple_of(g * rows_in, rows_in), rows_in), :]
-        got = lax.dot_general(
-            pick, h, (((0,), (0,)), ((), ())), preferred_element_type=jnp.float32
-        ).astype(jnp.bfloat16)
-        hpad[pl.ds(g * tiles_in, tiles_in)] = got.reshape(tiles_in, TILE, got.shape[1])
-        return carry
-
-    lax.fori_loop(0, n_groups, pad, 0)
-
-    i = lax.broadcasted_iota(jnp.int32, (rows, slots * TILE), 0)
-    j = lax.broadcasted_iota(jnp.int32, (rows, slots * TILE), 1)
-    turn = jnp.where((i % slots) * TILE + i // slots == j, 1.0, 0.0).astype(jnp.bfloat16)
-
-    def gather(n, carry):
-        part, k = lax.div(n, n_y), lax.rem(n, n_y)
-        owner = lax.rem(y + k, n_y) * 2 + lax.rem(c + 1 + part, 2)
-        for s in range(slots):
-            item = tab[owner * slots + s] // 256
-            tiles[s * TILE : (s + 1) * TILE, :] = hpad[item]
-        hperm[part, k] = jnp.dot(turn, tiles[...], preferred_element_type=jnp.float32).astype(
-            jnp.bfloat16
-        )
-        return carry
-
-    lax.fori_loop(0, 2 * n_y, gather, 0)
-
-    def project(b, part):
-        def one(k, carry):
-            w = head[...] if b == 0 else hw[b - 1]
-            pbuf[b, part, k] = jnp.dot(
-                hperm[part, k], w, preferred_element_type=jnp.float32
-            ).astype(jnp.bfloat16)
+
+    s_of = lax.broadcasted_iota(jnp.int32, (streams, items), 0)
+    lane = lax.broadcasted_iota(jnp.int32, (streams, items), 1)
+    mine = s_of == lane // TILE * per + lane % per
+    late = lane // per % 2 == 1
+
+    eye = lax.broadcasted_iota(jnp.int32, (streams, streams), 0) == lax.broadcasted_iota(
+        jnp.int32, (streams, streams), 1
+    )
+
+    def column(v):
+        return jnp.sum(jnp.where(eye, v, 0), axis=1, keepdims=True)
+
+    def along(first, later):
+        v = jnp.where(mine, jnp.where(late, later, first), 0)
+        return jnp.sum(v, axis=0, keepdims=True)
+
+    key = holder[...] * slots + position[...]
+    length = counts[...]
+    c0 = column(length[0:1])
+    keys = along(column(key[0:1]), column(key[1:2]))
+    lengths = along(c0, column(length[1:2]))
+
+    r = lax.broadcasted_iota(jnp.int32, (n_y * 2 * slots, items), 0)
+    core = (r // (n_y * slots) + c + 1) % 2
+    owner = (r // slots % n_y + y) % n_y * 2 + core
+    pick[...] = jnp.where(keys == owner * slots + r % slots, 1.0, 0.0).astype(jnp.bfloat16)
+
+    own_slot = lax.broadcasted_iota(jnp.int32, (slots, items), 0) + mi * slots
+    hit = keys == own_slot
+    count = jnp.sum(jnp.where(hit, lengths, 0), axis=1, keepdims=True)
+    is_late = lax.broadcasted_iota(jnp.int32, (slots, items), 1) // per % 2
+    second = jnp.sum(jnp.where(hit, is_late, 0), axis=1, keepdims=True) > 0
+
+    ri = lax.broadcasted_iota(jnp.int32, (rows - CTX * TILE, rows_in), 0)
+    ci = lax.broadcasted_iota(jnp.int32, (rows - CTX * TILE, rows_in), 1)
+    place = ri % per * seq + ri // per % 2 * half_seq + ri // TILE
+    main = jnp.where(ci == place, 1.0, 0.0).astype(jnp.bfloat16)
+    rc = lax.broadcasted_iota(jnp.int32, (CTX * TILE, rows_in), 0)
+    cc = lax.broadcasted_iota(jnp.int32, (CTX * TILE, rows_in), 1)
+
+    for g in range(groups):
+        back = jnp.concatenate([c0[g * per : (g + 1) * per]] * (CTX * 2), axis=0) - CTX + rc // TILE
+        hits = (cc == rc % per * seq + back) & (back >= 0) & (rc // per % 2 == 1)
+        sel[g, : CTX * TILE, :] = jnp.where(hits, 1.0, 0.0).astype(jnp.bfloat16)
+        sel[g, CTX * TILE :, :] = main
+
+    def project(w_ref, blocks):
+        n = len(blocks) * cols
+
+        def ordered(g, carry):
+            h = hid[pl.ds(pl.multiple_of(g * rows_in, rows_in), rows_in), :]
+            p = jnp.dot(h, w_ref[...], preferred_element_type=jnp.float32).astype(jnp.bfloat16)
+            q = jnp.dot(sel[g], p, preferred_element_type=jnp.float32).astype(jnp.bfloat16)
+            at = pl.ds(pl.multiple_of(g * TILE, TILE), TILE)
+            framed[:, at, :n] = q.reshape(frames, TILE, n)
             return carry
 
-        lax.fori_loop(0, n_y, one, 0)
-
-    project(0, 0)
-    project(0, 1)
+        def spread(t, carry):
+            v = jnp.dot(pick[...], framed[t, :, :n], preferred_element_type=jnp.float32)
+            v = v.astype(jnp.bfloat16)
+            at = pl.ds(pl.multiple_of(t * slots, slots), slots)
+            for i, b in enumerate(blocks):
+                part = v[:, i * cols : (i + 1) * cols]
+                pbuf[b, :, :, at, :] = part.reshape(2, n_y, slots, cols)
+            return carry
+
+        if blocks[0] == 0:
+            head_load.wait()
+            for n_load in range(LOADS):
+                loads[n_load].wait()
+                for g in range(groups // LOADS):
+                    ordered(n_load * (groups // LOADS) + g, 0)
+        else:
+            twice(groups, ordered, 4)
+        twice(frames, spread, 7)
+
+    project(head, (0,))
     pl.semaphore_wait(barrier, 8)
 
     def pair(b):
@@ -235,11 +289,18 @@
         q = xi if b == 0 else origin[b - 1]
         x[:, pl.ds(pl.multiple_of(q * cols, cols), cols)] = v.astype(jnp.bfloat16)
 
-    def head_in(j):
-        arrived(hw.at[j], head_s.at[j], head_r.at[j])
-        project(j + 1, 0)
-        pair(j + 1)
-        project(j + 1, 1)
+    def head_ref(j):
+        return hw1 if j == 2 else hw2.at[:, pl.ds(j * cols, cols)]
+
+    def head_send(j):
+        send(head, head_ref(j), head_s.at[j], head_r.at[j], across[j])
+
+    def head_in(*js):
+        for j in js:
+            arrived(head_ref(j), head_s.at[j], head_r.at[j])
+        project(hw1 if js == (2,) else hw2, tuple(j + 1 for j in js))
+        for j in js:
+            pair(j + 1)
 
     half, quarter = piece // 2, piece // 4
     e = lax.rem(zi, 2)
@@ -247,10 +308,9 @@
     def up_rows(q, offset, n):
         return wup.at[:, pl.ds(pl.multiple_of(q * piece + offset, n), n), :]
 
-    def upx_send():
+    def upx_send(j):
         mine = wupin.at[:, pl.ds(pl.multiple_of(c * half + e * quarter, quarter), quarter), :]
-        for j in range(3):
-            send(mine, up_rows(xi, c * half + e * quarter, quarter), upx_s.at[j], upx_r.at[j], across[j])
+        send(mine, up_rows(xi, c * half + e * quarter, quarter), upx_s.at[j], upx_r.at[j], across[j])
 
     def upx_in(j):
         at = c * half + e * quarter
@@ -270,46 +330,49 @@
     def upc_in(j):
         arrived(up_rows(origin[j], (1 - c) * half, half), upc_s.at[j], upc_r.at[j])
 
-    for j in range(3):
-        send(head, hw.at[j], head_s.at[j], head_r.at[j], across[j])
+    head_send(0)
+    head_send(1)
     pair(0)
     step(0, 0)
-    head_in(0)
-    head_in(1)
-    upx_send()
+    head_send(2)
+    head_in(0, 1)
+    upx_send(0)
+    upx_send(1)
     step(0, 1)
+    head_in(2)
+    upx_send(2)
     step(1, 0)
-    head_in(2)
     step(2, 0)
     step(0, 2)
+    step(3, 0)
     step(1, 1)
-    step(3, 0)
     step(2, 1)
     step(0, 3)
+    step(3, 1)
+    upx_in(0)
+    upx_in(1)
     step(1, 2)
-    step(3, 1)
     step(2, 2)
     final(0)
-    upx_in(0)
+    step(3, 2)
+    upx_in(2)
     step(1, 3)
-    step(3, 2)
     step(2, 3)
-    upx_in(1)
-    final(1)
-    step(3, 3)
-    upx_in(2)
     upz_in(0)
     upz_in(1)
+    step(3, 3)
+    final(1)
     final(2)
     upz_in(2)
     final(3)
     for j in range(3):
         upc_in(j)
-    own_up.wait()
+    for copy in others:
+        copy.wait()
     for copy in sent:
         copy.wait_send()
     vocode(
-        slots, frames, stride, lambda s: tab[mi * slots + s],
+        slots, frames, stride, count, second,
         x, wup, bias, a1, dw, a2, pw, out, up, act, out32,
     )
 
@@ -342,19 +405,6 @@
     depth, cols = latent_head_weight.shape
     latent = cols * n_x
 
-    item = jnp.arange(items, dtype=jnp.int32).reshape(streams, 2)
-    key = stretch_holder * slots + stretch_position
-    word = 1 + 2 * stretch_frame_count + 256 * item
-    place = jnp.arange(n_mp * slots, dtype=jnp.int32)
-    tab = jnp.sum(jnp.where(key[:, :, None] == place, word[:, :, None], 0), axis=(0, 1))
-    group = TILE // 2
-    j = jnp.arange(TILE, dtype=jnp.int32)[None, None, :]
-    st = (item % TILE)[:, :, None]
-    back = stretch_frame_count[:, 0:1, None] - CTX + j
-    back = jnp.where((item[:, :, None] % 2 == 1) & (back >= 0), (st // 2) * seq_len + back, -1)
-    here = jnp.where(j < frames, st * stretch_len + j - CTX, -1)
-    src = jnp.where(j < CTX, back, here).reshape(streams // group, 2 * group * TILE)
-
     vmem = pl.BlockSpec(memory_space=pltpu.VMEM)
     anywhere = pl.BlockSpec(memory_space=pl.ANY)
     bf16, f32 = jnp.bfloat16, jnp.float32
@@ -362,14 +412,18 @@
     out = pl.pallas_call(
         functools.partial(kernel, slots, frames, stride, n_z, n_y, n_x),
         out_shape=jax.ShapeDtypeStruct((slots, span, width), bf16),
-        in_specs=[pl.BlockSpec(memory_space=pltpu.SMEM), vmem, anywhere, vmem, anywhere] + [vmem] * 5,
+        in_specs=[vmem] * 6 + [anywhere] * 5,
         out_specs=vmem,
         scratch_shapes=[
             pltpu.VMEM(hidden.shape, bf16),
-            pltpu.VMEM((items, TILE, depth), bf16),
-            pltpu.VMEM((slots * TILE, depth), bf16),
-            pltpu.VMEM((2, n_y, rows, depth), bf16),
-            pltpu.VMEM((3, depth, cols), bf16),
+            pltpu.VMEM((depth, cols), bf16),
+            pltpu.VMEM(dilated_weight.shape, bf16),
+            pltpu.VMEM(pointwise_weight.shape, bf16),
+            pltpu.VMEM((items // TILE, rows, TILE // 2 * seq_len), bf16),
+            pltpu.VMEM((n_mp * slots, items), bf16),
+            pltpu.VMEM((frames, items, 2 * cols), bf16),
+            pltpu.VMEM((depth, 2 * cols), bf16),
+            pltpu.VMEM((depth, cols), bf16),
             pltpu.VMEM((BLOCKS, 2, n_y, rows, cols), bf16),
             pltpu.VMEM((BLOCKS, n_y, rows, cols), bf16),
             pltpu.VMEM((BLOCKS, 2, rows // 2, cols), bf16),
@@ -381,7 +435,7 @@
             pltpu.VMEM((stride, rows - CTX * slots, width), f32),
             pltpu.VMEM((stride, rows - slots, width), bf16),
             pltpu.VMEM((2, slots * span, width // 2), f32),
-            dma((2,)),
+            dma((LOADS + 4,)),
             dma((3,)), dma((3,)),
             dma((BLOCKS,)), dma((BLOCKS,)),
             dma((BLOCKS, 2, 4)), dma((BLOCKS, 2, 4)),
@@ -393,9 +447,9 @@
             collective_id=0, has_side_effects=True, vmem_limit_bytes=56 * 2**20
         ),
     )(
-        tab, src, hidden, latent_head_weight, upsample_weight,
-        upsample_bias[None], snake_alpha_first[None], dilated_weight,
-        snake_alpha_second[None], pointwise_weight,
+        stretch_holder.T, stretch_position.T, stretch_frame_count.T,
+        upsample_bias[None], snake_alpha_first[None], snake_alpha_second[None],
+        hidden, latent_head_weight, upsample_weight, dilated_weight, pointwise_weight,
     )
     return out.reshape(1, slots, 1, span, width)
 

time: 78 us -> 56.8 us (0.73)
  Pallas kernels: 72 us -> 54.6 us
  other arithmetic: 2.57 us -> 0 us
  local copies, waits for them, and re-layouts: 3.1 us -> 2.06 us
    pallas_call x1, Pallas kernels: 72 us -> 54.6 us  [body(): pl.pallas_call(functools.partial(kernel, slots, frames, stride, n_z, n_y,...]
    add x2 -> x0, other arithmetic: 0.79 us -> none  [the longest x1 0.72 us: body(): word = 1 + 2 * stretch_frame_count + 256 * item]
where the time goes in v3:
time: 56.8 us; the launch traced here: 56.7 us
  Pallas kernels  54.6 us (96%)
  local copies, waits for them, and re-layouts  2.06 us (4%)
    pallas_call x1, Pallas kernels, body(): pl.pallas_call(functools.partial(kernel, slots, frames, stride, n_z, n_y,...  54.6 us
    unnamed x1, local copies, waits for them, and re-layouts  2.06 us

profile of v3, /device:TPU:1, one launch (start us, length us, event | category | flops | bytes accessed | tf_op | source)
XLA Modules:
  0.0 56.7 jit_solution(10469359894607100110)
XLA Ops:
  0.0 54.6 %shard_map.109 = bf16[16,96,256]{2,1,0:T(8,128)(2,1)} custom-call(s32[2,64]{1,0:T(2,128)} %bitcast.10, s32[2,64]{1,0:T(2,128)} %bitcast.11, s32[2,64]{1,0:T(2,128)} %bitcast.12, f32[1,256]{1,0:T(1,128)} %bitcast.13, f32[1,256]{1,0:T(1,128)} %bitcast.14, f32[1,256]{1,0:T(1,128)} %bitcast.15, bf16[1536,512]{1,0:T(8,128)(2,1)} %hidden.1, ...), custom_call_target="tpu_custom_call" | custom-call | tf_op jit(solution)/shard_map/pallas_call | solution.py:412
  54.6 2.1 %copy.14 = bf16[1,16,1,96,256]{4,3,2,1,0:T(8,128)(2,1)} copy(bf16[1,16,1,96,256]{4,3,2,1,0:T(8,128)(2,1)} %bitcast.9) | data formatting | bytes 1572864

commit v4 on v3

--- a/solution.py
+++ b/solution.py
@@ -12,6 +12,7 @@
 TILE = 16
 BLOCKS = 4
 LOADS = 4
+EARLY = True
 MESH = pl.DeviceIdType.MESH
 
 SIN2 = (
@@ -35,6 +36,11 @@
 
 
 def twice(n, step, per=2):
+    if n == per:
+        for j in range(n):
+            step(j, 0)
+        return
+
     def some(i, carry):
         for j in range(per):
             step(per * i + j, carry)
@@ -53,31 +59,30 @@
     inv1 = 1.0 / a1[...]
     turns2 = a2[...] * (1.0 / jnp.pi)
     inv2 = 1.0 / a2[...]
-    x1 = x_ref[pl.ds(slots, rows - slots), :]
-    x0 = x_ref[pl.ds(0, rows - slots), :]
+    both = jnp.concatenate(
+        [x_ref[pl.ds(slots, rows - slots), :], x_ref[pl.ds(0, rows - slots), :]], axis=1
+    )
 
     def first(r, carry):
-        col = pl.ds(pl.multiple_of(r * width, width), width)
-        u = jnp.dot(x1, wup[0, :, col], preferred_element_type=jnp.float32)
-        u = u + jnp.dot(x0, wup[1, :, col], preferred_element_type=jnp.float32) + bias[...]
+        col = pl.ds(r * width, width)
+        w = jnp.concatenate([wup[0, :, col], wup[1, :, col]], axis=0)
+        u = jnp.dot(both, w, preferred_element_type=jnp.float32) + bias[...]
         u = jnp.concatenate([jnp.where(second, u[:slots], 0.0), u[slots:]], axis=0)
         up[r] = u[slots:]
         act[r] = snake(u, turns1, inv1).astype(jnp.bfloat16)
         return carry
 
-    twice(stride, first)
+    twice(stride, first, stride)
 
     def tap(r, back):
         s = r - back
-        same = s >= 0
-        which = jnp.where(same, s, s + stride)
-        start = pl.multiple_of(jnp.where(same, slots, 0), slots)
-        return act[which, pl.ds(start, live), :]
+        if s >= 0:
+            return act[s, pl.ds(slots, live), :]
+        return act[s + stride, pl.ds(0, live), :]
 
     def second_half(r, carry):
-        d = jnp.dot(tap(r, 0), dw[0], preferred_element_type=jnp.float32)
-        d = d + jnp.dot(tap(r, DILATION_RATE), dw[1], preferred_element_type=jnp.float32)
-        d = d + jnp.dot(tap(r, 2 * DILATION_RATE), dw[2], preferred_element_type=jnp.float32)
+        taps = jnp.concatenate([tap(r, j * DILATION_RATE) for j in range(3)], axis=1)
+        d = jnp.dot(taps, dw[...].reshape(3 * width, width), preferred_element_type=jnp.float32)
         b = snake(d, turns2, inv2).astype(jnp.bfloat16)
         o = up[r] + jnp.dot(b, pw[...], preferred_element_type=jnp.float32)
         for t in range(frames - CTX):
@@ -87,7 +92,7 @@
             out32[1, at, :] = piece[:, half:]
         return carry
 
-    twice(stride, second_half)
+    twice(stride, second_half, stride)
 
     def pack(s, carry):
         at = pl.ds(pl.multiple_of(s * span, span), span)
@@ -96,7 +101,7 @@
         )
         return carry
 
-    lax.fori_loop(0, slots, pack, 0)
+    twice(slots, pack, 4)
 
 
 def kernel(
@@ -104,7 +109,7 @@
     holder, position, counts, bias, a1, a2, hidden, headin, wupin, dwin, pwin,
     out,
     hid, head, dw, pw, sel, pick, framed, hw2, hw1, pbuf, sib, rx0, rx, tx0, tx, x, wup, up, act, out32,
-    local_sem, head_s, head_r, pair_s, pair_r, ring_s, ring_r, upx_s, upx_r, upz_s, upz_r, upc_s, upc_r,
+    local_sem, head_s, head_r, pair_s, pair_r, ring_s, ring_r, upx_s, upx_r, upf_s, upf_r, upz_s, upz_r, upc_s, upc_r,
 ):
     zi, mi, xi = lax.axis_index("pipe"), lax.axis_index("mp"), lax.axis_index("dp")
     y, c = lax.div(mi, 2), lax.rem(mi, 2)
@@ -220,17 +225,17 @@
         n = len(blocks) * cols
 
         def ordered(g, carry):
-            h = hid[pl.ds(pl.multiple_of(g * rows_in, rows_in), rows_in), :]
+            h = hid[pl.ds(g * rows_in, rows_in), :]
             p = jnp.dot(h, w_ref[...], preferred_element_type=jnp.float32).astype(jnp.bfloat16)
             q = jnp.dot(sel[g], p, preferred_element_type=jnp.float32).astype(jnp.bfloat16)
-            at = pl.ds(pl.multiple_of(g * TILE, TILE), TILE)
+            at = pl.ds(g * TILE, TILE)
             framed[:, at, :n] = q.reshape(frames, TILE, n)
             return carry
 
         def spread(t, carry):
             v = jnp.dot(pick[...], framed[t, :, :n], preferred_element_type=jnp.float32)
             v = v.astype(jnp.bfloat16)
-            at = pl.ds(pl.multiple_of(t * slots, slots), slots)
+            at = pl.ds(t * slots, slots)
             for i, b in enumerate(blocks):
                 part = v[:, i * cols : (i + 1) * cols]
                 pbuf[b, :, :, at, :] = part.reshape(2, n_y, slots, cols)
@@ -243,8 +248,8 @@
                 for g in range(groups // LOADS):
                     ordered(n_load * (groups // LOADS) + g, 0)
         else:
-            twice(groups, ordered, 4)
-        twice(frames, spread, 7)
+            twice(groups, ordered, groups)
+        twice(frames, spread, frames)
 
     project(head, (0,))
     pl.semaphore_wait(barrier, 8)
@@ -295,29 +300,36 @@
     def head_send(j):
         send(head, head_ref(j), head_s.at[j], head_r.at[j], across[j])
 
+    half, quarter = piece // 2, piece // 4
+    e = lax.rem(zi, 2)
+
+    def up_rows(q, offset, n):
+        return wup.at[:, pl.ds(pl.multiple_of(q * piece + offset, n), n), :]
+
+    def upx_send(j):
+        mine = wupin.at[:, pl.ds(pl.multiple_of(c * half + e * quarter, quarter), quarter), :]
+        send(mine, up_rows(xi, c * half + e * quarter, quarter), upx_s.at[j], upx_r.at[j], across[j])
+
     def head_in(*js):
         for j in js:
             arrived(head_ref(j), head_s.at[j], head_r.at[j])
+        for j in js:
+            if j < 2 and EARLY:
+                upx_send(j)
         project(hw1 if js == (2,) else hw2, tuple(j + 1 for j in js))
         for j in js:
             pair(j + 1)
 
-    half, quarter = piece // 2, piece // 4
-    e = lax.rem(zi, 2)
-
-    def up_rows(q, offset, n):
-        return wup.at[:, pl.ds(pl.multiple_of(q * piece + offset, n), n), :]
-
-    def upx_send(j):
-        mine = wupin.at[:, pl.ds(pl.multiple_of(c * half + e * quarter, quarter), quarter), :]
-        send(mine, up_rows(xi, c * half + e * quarter, quarter), upx_s.at[j], upx_r.at[j], across[j])
-
     def upx_in(j):
         at = c * half + e * quarter
-        arrived(up_rows(origin[j], at, quarter), upx_s.at[j], upx_r.at[j])
+        pieces = [up_rows(origin[j], at + d * (quarter // 2), quarter // 2) for d in range(2)]
+        if j < 2:
+            arrived(up_rows(origin[j], at, quarter), upx_s.at[j], upx_r.at[j])
+            send(pieces[j], pieces[j], upf_s.at[j], upf_r.at[j], across[j])
         for d in range(2):
-            ref = up_rows(origin[j], at + d * (quarter // 2), quarter // 2)
-            send(ref, ref, upz_s.at[j, d], upz_r.at[j, d], updown[d])
+            if j == 2:
+                arrived(pieces[d], upf_s.at[d], upf_r.at[d])
+            send(pieces[d], pieces[d], upz_s.at[j, d], upz_r.at[j, d], updown[d])
 
     def upz_in(j):
         at = c * half + (1 - e) * quarter
@@ -336,11 +348,8 @@
     step(0, 0)
     head_send(2)
     head_in(0, 1)
-    upx_send(0)
-    upx_send(1)
     step(0, 1)
     head_in(2)
-    upx_send(2)
     step(1, 0)
     step(2, 0)
     step(0, 2)
@@ -369,12 +378,12 @@
         upc_in(j)
     for copy in others:
         copy.wait()
-    for copy in sent:
-        copy.wait_send()
     vocode(
         slots, frames, stride, count, second,
         x, wup, bias, a1, dw, a2, pw, out, up, act, out32,
     )
+    for copy in sent:
+        copy.wait_send()
 
 
 def body(
@@ -439,7 +448,8 @@
             dma((3,)), dma((3,)),
             dma((BLOCKS,)), dma((BLOCKS,)),
             dma((BLOCKS, 2, 4)), dma((BLOCKS, 2, 4)),
-            dma((3,)), dma((3,)),
+            dma((2,)), dma((2,)),
+            dma((2,)), dma((2,)),
             dma((3, 2)), dma((3, 2)),
             dma((3,)), dma((3,)),
         ],

time: 56.8 us -> 54.9 us (0.967)
  Pallas kernels: 54.6 us -> 52.6 us
    pallas_call x1, Pallas kernels: 54.6 us -> 52.6 us  [body(): pl.pallas_call(functools.partial(kernel, slots, frames, stride, n_z, n_y,...]
where the time goes in v4:
time: 54.9 us; the launch traced here: 54.7 us
  Pallas kernels  52.6 us (96%)
  local copies, waits for them, and re-layouts  2.06 us (4%)
    pallas_call x1, Pallas kernels, body(): pl.pallas_call(functools.partial(kernel, slots, frames, stride, n_z, n_y,...  52.6 us
    unnamed x1, local copies, waits for them, and re-layouts  2.06 us

profile of v4, /device:TPU:1, one launch (start us, length us, event | category | flops | bytes accessed | tf_op | source)
XLA Modules:
  0.0 54.7 jit_solution(15428729539406620630)
XLA Ops:
  0.0 52.6 %shard_map.109 = bf16[16,96,256]{2,1,0:T(8,128)(2,1)} custom-call(s32[2,64]{1,0:T(2,128)} %bitcast.10, s32[2,64]{1,0:T(2,128)} %bitcast.11, s32[2,64]{1,0:T(2,128)} %bitcast.12, f32[1,256]{1,0:T(1,128)} %bitcast.13, f32[1,256]{1,0:T(1,128)} %bitcast.14, f32[1,256]{1,0:T(1,128)} %bitcast.15, bf16[1536,512]{1,0:T(8,128)(2,1)} %hidden.1, ...), custom_call_target="tpu_custom_call" | custom-call | tf_op jit(solution)/shard_map/pallas_call | solution.py:421
  52.6 2.1 %copy.14 = bf16[1,16,1,96,256]{4,3,2,1,0:T(8,128)(2,1)} copy(bf16[1,16,1,96,256]{4,3,2,1,0:T(8,128)(2,1)} %bitcast.9) | data formatting | bytes 1572864

commit v5 on v4

--- a/solution.py
+++ b/solution.py
@@ -95,13 +95,13 @@
     twice(stride, second_half, stride)
 
     def pack(s, carry):
-        at = pl.ds(pl.multiple_of(s * span, span), span)
+        at = pl.ds(s * span, span)
         out_ref[s] = jnp.concatenate([out32[0, at, :], out32[1, at, :]], axis=1).astype(
             out_ref.dtype
         )
         return carry
 
-    twice(slots, pack, 4)
+    twice(slots, pack, slots)
 
 
 def kernel(

time: 54.9 us -> 54.9 us (level)
  no operation moved by 1% of the time
where the time goes in v5:
time: 54.9 us; the launch traced here: 54.7 us
  Pallas kernels  52.7 us (96%)
  local copies, waits for them, and re-layouts  2.06 us (4%)
    pallas_call x1, Pallas kernels, body(): pl.pallas_call(functools.partial(kernel, slots, frames, stride, n_z, n_y,...  52.7 us
    unnamed x1, local copies, waits for them, and re-layouts  2.06 us

profile of v5, /device:TPU:1, one launch (start us, length us, event | category | flops | bytes accessed | tf_op | source)
XLA Modules:
  0.0 54.7 jit_solution(13141406631604079512)
XLA Ops:
  0.0 52.7 %shard_map.109 = bf16[16,96,256]{2,1,0:T(8,128)(2,1)} custom-call(s32[2,64]{1,0:T(2,128)} %bitcast.10, s32[2,64]{1,0:T(2,128)} %bitcast.11, s32[2,64]{1,0:T(2,128)} %bitcast.12, f32[1,256]{1,0:T(1,128)} %bitcast.13, f32[1,256]{1,0:T(1,128)} %bitcast.14, f32[1,256]{1,0:T(1,128)} %bitcast.15, bf16[1536,512]{1,0:T(8,128)(2,1)} %hidden.1, ...), custom_call_target="tpu_custom_call" | custom-call | tf_op jit(solution)/shard_map/pallas_call | solution.py:421
  52.7 2.1 %copy.14 = bf16[1,16,1,96,256]{4,3,2,1,0:T(8,128)(2,1)} copy(bf16[1,16,1,96,256]{4,3,2,1,0:T(8,128)(2,1)} %bitcast.9) | data formatting | bytes 1572864
